TPU v7x, 256 devices: a whole 4x4x8 slice. The times are simulated.
256 devices in a mesh: sp: 16 (over x, y), blk: 16 (over z, core).
Axes of the slice: x: 4, y: 4, z: 8, core: 2. Of those that a mesh axis runs over, the one named last changes fastest.
Arguments:
- queries: bfloat16 [32768, 8192], P(('blk', 'sp')), may hold values from -120 to 120
- key_state_rows: bfloat16 [32768, 1024], P(('blk', 'sp')), may hold values from -6 to 6
- value_state_rows: bfloat16 [32768, 1024], P(('blk', 'sp')), may hold values from -6 to 6
- cotangent: bfloat16 [32768, 8192], P(('blk', 'sp')), may hold values from -6 to 6
- block_list: int32 [256, 1], replicated, may hold values from 0 to 255, as said below
- query_exponent: int32 [256, 64], P('blk'), may hold values from -5 to 1
- key_block_exponent: int32 [256, 8], P('blk'), may hold values from -5 to 1
- value_block_exponent: int32 [256, 8], P('blk'), may hold values from -5 to 1
Outputs:
- attention: bfloat16 [32768, 8192], P(('blk', 'sp'))
- query_gradient_rows: bfloat16 [32768, 8192], P(('blk', 'sp'))
- key_gradient_rows: bfloat16 [32768, 1024], P(('blk', 'sp'))
- value_gradient_rows: bfloat16 [32768, 1024], P(('blk', 'sp'))
Inputs may be any that keep to these rules, and one draw needn't show every extreme that they name: Each entry of block_list is the block of its own row or an earlier block. `block_list`: group the query blocks 16 at a time in order (the blocks held along one index of blk). Among the 16 entries of one group, at most 2 name blocks of any one other group and differ from their own row's block; in every draw some pair of groups reaches 2.
All inputs are finite; a program needn't handle non-finite values.
Results may differ from a plain program's by a relative error of at most 0.012.
Values may be sent and summed in bfloat16 or wider, within the bound.
No kernel may reach another device: no remote copies, remote signals or barrier semaphores. Data moves between devices by JAX's collectives and lax.ppermute only.
A program may use at most 128 MiB of HBM per device.

v0:
```python
import math

import jax
import jax.numpy as jnp
from jax import lax
from jax.sharding import PartitionSpec as P

QUERY_HEAD_COUNT = 64
KEY_VALUE_HEADS = 8
HEAD_SIZE = 128
BLOCK = 128
LIST = 1
CAP = 2


MAX_CODE = 448.0


def hadamard_table(order_n):
    indices = lax.iota(jnp.int32, order_n)
    common = jnp.bitwise_and(indices[:, None], indices[None, :])
    parity = jnp.zeros((order_n, order_n), jnp.int32)
    for bit_pos in range(order_n.bit_length() - 1):
        parity = parity + jnp.bitwise_and(jnp.right_shift(common, bit_pos), 1)
    return jnp.where(jnp.bitwise_and(parity, 1) == 0, 1.0, -1.0).astype(jnp.float32)


def quantize_rotated(states, exponent, hadamard_half):
    rotated = jnp.einsum("...d,de->...e", states, hadamard_half, preferred_element_type=jnp.float32)
    factor = jnp.exp2(exponent.astype(jnp.float32))
    coded = jnp.clip(rotated / factor, -MAX_CODE, MAX_CODE).astype(jnp.bfloat16)
    coded = lax.optimization_barrier(coded)
    return (coded.astype(jnp.float32) * factor).astype(jnp.bfloat16)


def local(
    queries,
    key_state_rows,
    value_state_rows,
    cotangent,
    block_list,
    query_exponent,
    key_block_exponent,
    value_block_exponent,
):
    token_rows = queries.shape[0]
    sparse_count = lax.axis_size("sp")
    blk_count = lax.axis_size("blk")
    sp_index = lax.axis_index("sp")
    blk_index = lax.axis_index("blk")
    copy_count = max(sparse_count, KEY_VALUE_HEADS)
    repeat_count = copy_count // KEY_VALUE_HEADS
    heads_local = QUERY_HEAD_COUNT // sparse_count
    pair_local = copy_count // sparse_count
    group_local = heads_local // pair_local
    hadamard_matrix = hadamard_table(HEAD_SIZE)
    hadamard_half = hadamard_matrix.astype(jnp.bfloat16)
    score_scale = 1.0 / (HEAD_SIZE * math.sqrt(HEAD_SIZE))
    pair_input = jnp.stack(
        [
            key_state_rows.reshape(token_rows, KEY_VALUE_HEADS, HEAD_SIZE),
            value_state_rows.reshape(token_rows, KEY_VALUE_HEADS, HEAD_SIZE),
        ],
        axis=2,
    )
    pair_split = jnp.repeat(pair_input, repeat_count, axis=1).reshape(
        token_rows, sparse_count, pair_local * 2 * HEAD_SIZE
    )
    query_split = queries.reshape(token_rows, sparse_count, heads_local * HEAD_SIZE)
    grad_split = cotangent.reshape(token_rows, sparse_count, heads_local * HEAD_SIZE)
    query_heads, pair_heads = (
        lax.all_to_all(query_split, "sp", split_axis=1, concat_axis=0, tiled=True),
        lax.all_to_all(pair_split, "sp", split_axis=1, concat_axis=0, tiled=True),
    )
    head_rows = query_heads.shape[0]
    blocks_dev = head_rows // BLOCK
    key_count = (1 + LIST) * BLOCK
    query_power = lax.dynamic_slice_in_dim(query_exponent, sp_index * heads_local, heads_local, 1)
    pair_ids = (sp_index * pair_local + jnp.arange(pair_local, dtype=jnp.int32)) // repeat_count
    pair_power = jnp.stack(
        [
            jnp.take(key_block_exponent, pair_ids, axis=1),
            jnp.take(value_block_exponent, pair_ids, axis=1),
        ],
        axis=2,
    )
    query_lead = jnp.transpose(
        query_heads.reshape(blocks_dev, BLOCK, heads_local, HEAD_SIZE), (0, 2, 1, 3)
    )
    query_deq = quantize_rotated(query_lead, query_power[:, :, None, None], hadamard_half)
    pair_lead = jnp.transpose(
        pair_heads.reshape(blocks_dev, BLOCK, pair_local, 2, HEAD_SIZE), (0, 2, 3, 1, 4)
    )
    pair_deq = quantize_rotated(pair_lead, pair_power[:, :, :, None, None], hadamard_half)
    entries = blocks_dev * LIST
    listed = block_list.reshape(blk_count, entries)
    own_ids = jnp.repeat(jnp.arange(blk_count * blocks_dev, dtype=jnp.int32), LIST).reshape(
        blk_count, entries
    )
    owners = listed // blocks_dev
    requester_ids = jnp.arange(blk_count, dtype=jnp.int32)
    remote = (listed != own_ids) & (owners != requester_ids[:, None])
    slot_ids = jnp.arange(entries, dtype=jnp.int32)
    before = (
        (owners[:, :, None] == owners[:, None, :])
        & remote[:, None, :]
        & (slot_ids[None, None, :] < slot_ids[None, :, None])
    )
    slot_rank = jnp.sum(before.astype(jnp.int32), axis=2)
    cap_ids = jnp.arange(CAP, dtype=jnp.int32)
    serves = (
        remote[:, None, :]
        & (owners[:, None, :] == blk_index)
        & (slot_rank[:, None, :] == cap_ids[None, :, None])
    )
    serve_valid = jnp.any(serves, axis=2).reshape(-1)
    serve_block = jnp.sum(
        jnp.where(serves, listed[:, None, :] - blk_index * blocks_dev, 0), axis=2
    ).reshape(-1)
    my_listed = lax.dynamic_index_in_dim(listed, blk_index, 0, keepdims=False)
    my_owner = lax.dynamic_index_in_dim(owners, blk_index, 0, keepdims=False)
    my_rank = lax.dynamic_index_in_dim(slot_rank, blk_index, 0, keepdims=False)
    my_remote = lax.dynamic_index_in_dim(remote, blk_index, 0, keepdims=False)
    outgoing = jnp.take(pair_deq, serve_block, axis=0)
    outgoing = jnp.where(serve_valid[:, None, None, None, None], outgoing, jnp.zeros_like(outgoing))
    outgoing = outgoing.reshape(blk_count, CAP, pair_local, 2, BLOCK, HEAD_SIZE)
    incoming = lax.all_to_all(outgoing, "blk", split_axis=0, concat_axis=0, tiled=True).reshape(
        blk_count * CAP, pair_local, 2, BLOCK, HEAD_SIZE
    )
    remote_pick = jnp.take(incoming, my_owner * CAP + jnp.minimum(my_rank, CAP - 1), axis=0)
    local_index = jnp.clip(my_listed - blk_index * blocks_dev, 0, blocks_dev - 1)
    local_pick = jnp.take(pair_deq, local_index, axis=0)
    entry_pairs = jnp.where(my_remote[:, None, None, None, None], remote_pick, local_pick)
    entry_pairs = entry_pairs.reshape(blocks_dev, LIST, pair_local, 2, BLOCK, HEAD_SIZE)
    my_blocks = my_listed.reshape(blocks_dev, LIST)
    own_block = blk_index * blocks_dev + jnp.arange(blocks_dev, dtype=jnp.int32)
    earlier_tri = jnp.arange(LIST)[None, :] < jnp.arange(LIST)[:, None]
    repeated = jnp.any((my_blocks[:, :, None] == my_blocks[:, None, :]) & earlier_tri[None], axis=2)
    entry_ok = (my_blocks != own_block[:, None]) & jnp.logical_not(repeated)
    key_pairs = jnp.concatenate([pair_deq[:, None], entry_pairs], axis=1)
    key_part = jnp.transpose(key_pairs[:, :, :, 0], (0, 2, 1, 3, 4)).reshape(
        blocks_dev, pair_local, key_count, HEAD_SIZE
    )
    value_part = jnp.transpose(key_pairs[:, :, :, 1], (0, 2, 1, 3, 4)).reshape(
        blocks_dev, pair_local, key_count, HEAD_SIZE
    )
    causal = jnp.arange(BLOCK)[None, :] <= jnp.arange(BLOCK)[:, None]
    listed_cols = jnp.broadcast_to(
        jnp.repeat(entry_ok, BLOCK, axis=1)[:, None, :], (blocks_dev, BLOCK, LIST * BLOCK)
    )
    allowed = jnp.concatenate(
        [jnp.broadcast_to(causal[None], (blocks_dev, BLOCK, BLOCK)), listed_cols], axis=2
    )
    query_five = query_deq.reshape(blocks_dev, pair_local, group_local, BLOCK, HEAD_SIZE)
    scores = (
        jnp.einsum("bmgqd,bmkd->bmgqk", query_five, key_part, preferred_element_type=jnp.float32)
        * score_scale
    )
    masked = jnp.where(allowed[:, None, None], scores, -jnp.inf)
    row_max = jnp.max(masked, axis=-1, keepdims=True)
    weights = jnp.exp(masked - row_max)
    probability = weights / jnp.sum(weights, axis=-1, keepdims=True)
    probs_half = probability.astype(jnp.bfloat16)
    out_rot = jnp.einsum(
        "bmgqk,bmkd->bmgqd", probs_half, value_part, preferred_element_type=jnp.float32
    )
    attention_heads = (
        jnp.dot(out_rot.reshape(-1, HEAD_SIZE), hadamard_matrix, precision=lax.Precision.HIGHEST)
        / HEAD_SIZE
    ).astype(jnp.bfloat16)
    attention_heads = jnp.transpose(
        attention_heads.reshape(blocks_dev, pair_local, group_local, BLOCK, HEAD_SIZE),
        (0, 3, 1, 2, 4),
    ).reshape(head_rows, heads_local * HEAD_SIZE)

    def to_tokens(array):
        return array.reshape(sparse_count, token_rows, 1, array.shape[-1])

    attention = lax.all_to_all(
        to_tokens(attention_heads), "sp", split_axis=0, concat_axis=2, tiled=True
    ).reshape(token_rows, QUERY_HEAD_COUNT * HEAD_SIZE)
    grad_heads = lax.all_to_all(grad_split, "sp", split_axis=1, concat_axis=0, tiled=True)
    grad_lead = jnp.transpose(
        grad_heads.reshape(blocks_dev, BLOCK, heads_local, HEAD_SIZE), (0, 2, 1, 3)
    )
    grad_rot = (
        jnp.dot(grad_lead.reshape(-1, HEAD_SIZE), hadamard_half, preferred_element_type=jnp.float32)
        / HEAD_SIZE
    ).astype(jnp.bfloat16)
    grad_rot = grad_rot.reshape(blocks_dev, pair_local, group_local, BLOCK, HEAD_SIZE)
    row_delta = jnp.sum(grad_rot.astype(jnp.float32) * out_rot, axis=-1)
    prob_grad = jnp.einsum(
        "bmgqd,bmkd->bmgqk", grad_rot, value_part, preferred_element_type=jnp.float32
    )
    score_grad = probability * (prob_grad - row_delta[..., None])
    score_half = (score_grad * score_scale).astype(jnp.bfloat16)
    query_rot = jnp.einsum(
        "bmgqk,bmkd->bmgqd", score_half, key_part, preferred_element_type=jnp.float32
    )
    query_grad_heads = jnp.dot(
        query_rot.reshape(-1, HEAD_SIZE), hadamard_matrix, precision=lax.Precision.HIGHEST
    ).astype(jnp.bfloat16)
    query_grad_heads = jnp.transpose(
        query_grad_heads.reshape(blocks_dev, pair_local, group_local, BLOCK, HEAD_SIZE),
        (0, 3, 1, 2, 4),
    ).reshape(head_rows, heads_local * HEAD_SIZE)
    key_sums = jnp.einsum(
        "bmgqk,bmgqd->bmkd", score_half, query_five, preferred_element_type=jnp.float32
    )
    value_sums = jnp.einsum(
        "bmgqk,bmgqd->bmkd", probs_half, grad_rot, preferred_element_type=jnp.float32
    )
    pair_grad = jnp.stack([key_sums, value_sums], axis=2).reshape(
        blocks_dev, pair_local, 2, 1 + LIST, BLOCK, HEAD_SIZE
    )
    pair_grad = jnp.transpose(pair_grad, (0, 3, 1, 2, 4, 5))
    feature = pair_local * 2 * BLOCK * HEAD_SIZE
    diagonal = pair_grad[:, 0].reshape(blocks_dev, feature)
    entry_grads = (
        pair_grad[:, 1:].astype(jnp.bfloat16).reshape(entries, pair_local, 2, BLOCK, HEAD_SIZE)
    )
    back_match = (
        my_remote[None, None, :]
        & (my_owner[None, None, :] == requester_ids[:, None, None])
        & (my_rank[None, None, :] == cap_ids[None, :, None])
    )
    back_valid = jnp.any(back_match, axis=2).reshape(-1)
    back_index = jnp.sum(jnp.where(back_match, slot_ids[None, None, :], 0), axis=2).reshape(-1)
    returning = jnp.take(entry_grads, back_index, axis=0)
    returning = jnp.where(
        back_valid[:, None, None, None, None], returning, jnp.zeros_like(returning)
    )
    returning = returning.reshape(blk_count, CAP, pair_local, 2, BLOCK, HEAD_SIZE)
    received = lax.all_to_all(returning, "blk", split_axis=0, concat_axis=0, tiled=True).reshape(
        blk_count * CAP, feature
    )
    block_ids = jnp.arange(blocks_dev, dtype=jnp.int32)
    local_onehot = (local_index[None, :] == block_ids[:, None]) & jnp.logical_not(my_remote)[
        None, :
    ]
    recv_onehot = (serve_block[None, :] == block_ids[:, None]) & serve_valid[None, :]
    combined = diagonal + jnp.dot(
        local_onehot.astype(jnp.bfloat16),
        entry_grads.reshape(entries, feature),
        preferred_element_type=jnp.float32,
    )
    combined = combined + jnp.dot(
        recv_onehot.astype(jnp.bfloat16), received, preferred_element_type=jnp.float32
    )
    pair_duplicate = jnp.dot(
        combined.reshape(-1, HEAD_SIZE), hadamard_matrix, precision=lax.Precision.HIGHEST
    ).astype(jnp.bfloat16)
    pair_duplicate = jnp.transpose(
        pair_duplicate.reshape(blocks_dev, pair_local, 2, BLOCK, HEAD_SIZE), (0, 3, 1, 2, 4)
    ).reshape(head_rows, pair_local * 2 * HEAD_SIZE)
    query_grad, pair_backward = (
        lax.all_to_all(to_tokens(query_grad_heads), "sp", split_axis=0, concat_axis=2, tiled=True),
        lax.all_to_all(to_tokens(pair_duplicate), "sp", split_axis=0, concat_axis=2, tiled=True),
    )
    summed_rows = jnp.sum(
        pair_backward.reshape(token_rows, KEY_VALUE_HEADS, repeat_count, 2, HEAD_SIZE).astype(
            jnp.float32
        ),
        axis=2,
    ).astype(jnp.bfloat16)
    key_gradient_rows = summed_rows[:, :, 0].reshape(token_rows, KEY_VALUE_HEADS * HEAD_SIZE)
    value_gradient_rows = summed_rows[:, :, 1].reshape(token_rows, KEY_VALUE_HEADS * HEAD_SIZE)
    return (
        attention,
        query_grad.reshape(token_rows, QUERY_HEAD_COUNT * HEAD_SIZE),
        key_gradient_rows,
        value_gradient_rows,
    )


def solution(mesh):
    return jax.shard_map(
        local,
        mesh=mesh,
        in_specs=(
            P(("blk", "sp"), None),
            P(("blk", "sp"), None),
            P(("blk", "sp"), None),
            P(("blk", "sp"), None),
            P(),
            P("blk", None),
            P("blk", None),
            P("blk", None),
        ),
        out_specs=(
            P(("blk", "sp"), None),
            P(("blk", "sp"), None),
            P(("blk", "sp"), None),
            P(("blk", "sp"), None),
        ),
        check_vma=False,
    )
```

profile of v0, /device:TPU:1, one launch (start us, length us, event | category | flops | bytes accessed | tf_op | source)
XLA Modules:
  0.0 339.9 jit_solution(6559285363597767260)
XLA Ops:
  4.3 7.7 %all-to-all-start.1 = ((bf16[128,16,256]{0,2,1:T(8,128)(2,1)}), bf16[128,16,256]{0,2,1:T(8,128)(2,1)S(1)}, u32[]{:S(2)}, u32[]{:S(2)}) async-start(bf16[128,16,256]{0,2,1:T(8,128)(2,1)} %bitcast.8), calls=%async_computation.1 | async-start | bytes 2097152 | tf_op jit(solution)/shard_map/all_to_all | solution.py:73
  12.0 2.4 copy.145
  14.5 13.1 %all-to-all-done.1 = bf16[128,16,256]{0,2,1:T(8,128)(2,1)S(1)} async-done(((bf16[128,16,256]{0,2,1:T(8,128)(2,1)}), bf16[128,16,256]{0,2,1:T(8,128)(2,1)S(1)}, u32[]{:S(2)}, u32[]{:S(2)}) %all-to-all-start.1) | async-done | bytes 1048608 | tf_op jit(solution)/shard_map/all_to_all | solution.py:73
  27.5 4.1 %all-to-all-start.4 = ((bf16[128,16,512]{0,2,1:T(8,128)(2,1)}), bf16[128,16,512]{0,2,1:T(8,128)(2,1)S(1)}, u32[]{:S(2)}, u32[]{:S(2)}) async-start(bf16[128,16,512]{0,2,1:T(8,128)(2,1)} %bitcast.221), calls=%async_computation.4 | async-start | bytes 4194304 | tf_op jit(solution)/shard_map/all_to_all | solution.py:182
  32.9 4.1 %copy.130 = bf16[128,8192]{0,1:T(8,128)(2,1)} copy(bf16[128,8192]{1,0:T(8,128)(2,1)} %param.12) | data formatting | bytes 4194304 | tf_op args[0]
  38.3 18.7 %all-to-all-done.4 = bf16[128,16,512]{0,2,1:T(8,128)(2,1)S(1)} async-done(((bf16[128,16,512]{0,2,1:T(8,128)(2,1)}), bf16[128,16,512]{0,2,1:T(8,128)(2,1)S(1)}, u32[]{:S(2)}, u32[]{:S(2)}) %all-to-all-start.4) | async-done | bytes 2097184 | tf_op jit(solution)/shard_map/all_to_all | solution.py:182
  58.3 6.3 %all-to-all-start = ((bf16[128,16,512]{0,2,1:T(8,128)(2,1)}), bf16[128,16,512]{0,2,1:T(8,128)(2,1)}, u32[]{:S(2)}, u32[]{:S(2)}) async-start(bf16[128,16,512]{0,2,1:T(8,128)(2,1)} %bitcast.222), calls=%async_computation | async-start | bytes 4194304 | tf_op jit(solution)/shard_map/all_to_all | solution.py:72
  69.1 1.7 fusion.11
  70.8 18.9 %all-to-all-done = bf16[128,16,512]{0,2,1:T(8,128)(2,1)} async-done(((bf16[128,16,512]{0,2,1:T(8,128)(2,1)}), bf16[128,16,512]{0,2,1:T(8,128)(2,1)}, u32[]{:S(2)}, u32[]{:S(2)}) %all-to-all-start) | async-done | bytes 2097184 | tf_op jit(solution)/shard_map/all_to_all | solution.py:72
  89.7 15.3 %all-to-all-start.2 = ((bf16[16,2,1,2,128,128]{5,4,3,1,2,0:T(8,128)(2,1)}), bf16[16,2,1,2,128,128]{5,4,3,1,2,0:T(8,128)(2,1)}, u32[]{:S(2)}, u32[]{:S(2)}) async-start(bf16[16,2,1,2,128,128]{5,4,3,1,2,0:T(8,128)(2,1)} %bitcast.32), calls=%async_computation.2 | async-start | bytes 4194304 | tf_op jit(solution)/shard_map/all_to_all | solution.py:127
  106.9 1.7 gather_fusion.1
  108.6 2.6 copy.146
  111.2 3.7 %fusion.4 = bf16[8192,128]{0,1:T(8,128)(2,1)} fusion(bf16[8192,128]{1,0:T(8,128)(2,1)} %bitcast.226), kind=kOutput, calls=%fused_computation.12 | convolution fusion | flops 270942208 | bytes 4194304 | tf_op jit(solution)/shard_map/dot_general | solution.py:187
  114.9 3.2 copy.147
  118.1 3.9 %copy.131 = bf16[16,128,4,128]{3,1,2,0:T(8,128)(2,1)} copy(bf16[16,128,4,128]{1,3,2,0:T(8,128)(2,1)} %bitcast.5) | data formatting | bytes 4194304 | tf_op jit(solution)/shard_map/reshape | solution.py:88
  122.0 3.8 %fusion.15 = bf16[16,4,128,128]{2,3,1,0:T(8,128)(2,1)} fusion(f32[16,4]{1,0:T(8,128)S(1)} %multiply_exponential_fusion, bf16[16,128,4,128]{3,1,2,0:T(8,128)(2,1)} %copy.131), kind=kOutput, calls=%fused_computation.41 | convolution fusion | flops 271990784 | bytes 4194560 | tf_op jit(solution)/shard_map/...d,de->...e/dot_general | solution.py:29
  125.8 28.1 %all-to-all-done.2 = bf16[16,2,1,2,128,128]{5,4,3,1,2,0:T(8,128)(2,1)} async-done(((bf16[16,2,1,2,128,128]{5,4,3,1,2,0:T(8,128)(2,1)}), bf16[16,2,1,2,128,128]{5,4,3,1,2,0:T(8,128)(2,1)}, u32[]{:S(2)}, u32[]{:S(2)}) %all-to-all-start.2) | async-done | bytes 2097184 | tf_op jit(solution)/shard_map/all_to_all | solution.py:127
  153.9 3.2 gather_fusion
  159.1 1.8 copy-done.5
  160.9 4.8 %fusion.14 = f32[16,4,128,256]{3,2,1,0:T(8,128)} fusion(bf16[16,256,128,1]{2,1,3,0:T(8,128)(2,1)S(1)} %bitcast.218, bf16[16,4,128,128]{2,3,1,0:T(8,128)(2,1)S(1)} %copy-done.5, f32[16,4]{1,0:T(8,128)S(1)} %multiply_exponential_fusion), kind=kOutput, calls=%fused_computation.40 | convolution fusion | flops 540016640 | bytes 11534592 | tf_op jit(solution)/shard_map/bmgqd,bmkd->bmgqk/dot_general | solution.py:156
  165.7 10.2 %fusion.126 = (f32[16,4,128]{2,1,0:T(4,128)S(1)}, f32[16,4,128,256]{3,2,1,0:T(8,128)S(1)}) fusion(f32[16,4,128,256]{3,2,1,0:T(8,128)} %fusion.14, pred[16,128,256]{2,1,0:T(8,128)(4,1)} %pad_add_fusion), kind=kOutput, calls=%fused_computation.197 | output fusion | flops 12583167 | bytes 17334272 | tf_op jit(solution)/shard_map/sub | solution.py:161
  177.2 1.9 copy-done.7
  181.1 4.8 %fusion.3 = bf16[8192,128]{1,0:T(8,128)(2,1)} fusion(f32[8192,128]{1,0:T(8,128)S(1)} %bitcast.211), kind=kOutput, calls=%fused_computation.10 | convolution fusion | flops 1613103104 | bytes 6291456 | tf_op jit(solution)/shard_map/dot_general | solution.py:168
  185.9 3.9 %copy.143 = bf16[16,1,4,128,128]{3,4,2,0,1:T(8,128)(2,1)} copy(bf16[16,1,4,128,128]{4,3,2,0,1:T(8,128)(2,1)} %bitcast.216) | data formatting | bytes 4194304 | tf_op jit(solution)/shard_map/reshape | solution.py:172
  189.8 4.4 %all-to-all-start.3 = ((bf16[16,128,1,512]{1,3,2,0:T(8,128)(2,1)}), bf16[16,128,1,512]{1,3,2,0:T(8,128)(2,1)}, u32[]{:S(2)}, u32[]{:S(2)}) async-start(bf16[16,128,1,512]{1,3,2,0:T(8,128)(2,1)} %bitcast.224), calls=%async_computation.3 | async-start | bytes 4194304 | tf_op jit(solution)/shard_map/all_to_all | solution.py:179
  194.3 6.0 %multiply_convert_fusion = bf16[16,4,128,256]{3,2,1,0:T(8,128)(2,1)S(1)} fusion(f32[16,4,128]{2,1,0:T(4,128)S(1)} %get-tuple-element.58, f32[16,4,128,256]{3,2,1,0:T(8,128)} %copy-done.7, f32[16,4,128]{2,1,0:T(4,128)S(1)} %get-tuple-element.56, bf16[16,4,128,128]{3,2,1,0:T(8,128)(2,1)S(1)} %bitcast.214, bf16[16,256,128,1]{2,1,3,0:T(8,128)(2,1)} %bitcast.232), kind=kOutput, calls=%fused_computation.13 | convolution fusion | flops 547356672 | bytes 15794176 | tf_op jit(solution)/shard_map/bmgqd,bmkd->bmgqk/dot_general | solution.py:192
  203.4 1.7 fusion.13
  205.4 1.9 copy-done.3
  207.5 2.1 gather_fusion.3
  209.7 3.2 fusion.10
  212.9 10.6 %all-to-all-done.3 = bf16[16,128,1,512]{1,3,2,0:T(8,128)(2,1)} async-done(((bf16[16,128,1,512]{1,3,2,0:T(8,128)(2,1)}), bf16[16,128,1,512]{1,3,2,0:T(8,128)(2,1)}, u32[]{:S(2)}, u32[]{:S(2)}) %all-to-all-start.3) | async-done | bytes 2097184 | tf_op jit(solution)/shard_map/all_to_all | solution.py:179
  223.5 6.8 %all-to-all-start.6 = ((bf16[16,2,1,2,128,128]{5,4,3,1,2,0:T(8,128)(2,1)}), bf16[16,2,1,2,128,128]{5,4,3,1,2,0:T(8,128)(2,1)}, u32[]{:S(2)}, u32[]{:S(2)}) async-start(bf16[16,2,1,2,128,128]{5,4,3,1,2,0:T(8,128)(2,1)} %bitcast.90), calls=%async_computation.6 | async-start | bytes 4194304 | tf_op jit(solution)/shard_map/all_to_all | solution.py:234
  230.3 3.4 %fusion.127 = f32[16,4,128,128]{3,2,1,0:T(8,128)S(1)} fusion(bf16[16,4,128,256]{3,2,1,0:T(8,128)(2,1)} %copy-done.2, bf16[16,256,128,1]{2,1,3,0:T(8,128)(2,1)S(1)} %bitcast.219), kind=kOutput, calls=%fused_computation.199 | convolution fusion | flops 536870912 | bytes 9437184 | tf_op jit(solution)/shard_map/bmgqk,bmkd->bmgqd/dot_general | solution.py:197
  233.7 3.7 %convolution_convert_fusion = bf16[8192,128]{1,0:T(8,128)(2,1)S(1)} fusion(f32[8192,128]{1,0:T(8,128)S(1)} %bitcast.212), kind=kOutput, calls=%fused_computation.11 | convolution fusion | flops 1612054528 | bytes 6291456 | tf_op jit(solution)/shard_map/dot_general | solution.py:200
  237.4 2.6 copy.148
  240.0 39.3 %all-to-all-done.6 = bf16[16,2,1,2,128,128]{5,4,3,1,2,0:T(8,128)(2,1)} async-done(((bf16[16,2,1,2,128,128]{5,4,3,1,2,0:T(8,128)(2,1)}), bf16[16,2,1,2,128,128]{5,4,3,1,2,0:T(8,128)(2,1)}, u32[]{:S(2)}, u32[]{:S(2)}) %all-to-all-start.6) | async-done | bytes 2097184 | tf_op jit(solution)/shard_map/all_to_all | solution.py:234
  279.3 4.7 %all-to-all-start.5 = ((bf16[16,128,1,512]{1,3,2,0:T(8,128)(2,1)}), bf16[16,128,1,512]{1,3,2,0:T(8,128)(2,1)}, u32[]{:S(2)}, u32[]{:S(2)}) async-start(bf16[16,128,1,512]{1,3,2,0:T(8,128)(2,1)} %bitcast.223), calls=%async_computation.5 | async-start | bytes 4194304 | tf_op jit(solution)/shard_map/all_to_all | solution.py:257
  284.0 2.2 copy-done.4
  290.6 2.8 reshape.579
  295.2 1.7 fusion.1
  297.0 1.7 reshape.580
  298.7 1.8 convolution_convert_fusion.1
  301.9 11.4 %all-to-all-done.5 = bf16[16,128,1,512]{1,3,2,0:T(8,128)(2,1)} async-done(((bf16[16,128,1,512]{1,3,2,0:T(8,128)(2,1)}), bf16[16,128,1,512]{1,3,2,0:T(8,128)(2,1)}, u32[]{:S(2)}, u32[]{:S(2)}) %all-to-all-start.5) | async-done | bytes 2097184 | tf_op jit(solution)/shard_map/all_to_all | solution.py:257
  313.3 5.0 %all-to-all-start.7 = ((bf16[16,128,1,256]{1,3,2,0:T(8,128)(2,1)}), bf16[16,128,1,256]{1,3,2,0:T(8,128)(2,1)S(1)}, u32[]{:S(2)}, u32[]{:S(2)}) async-start(bf16[16,128,1,256]{1,3,2,0:T(8,128)(2,1)} %bitcast.94), calls=%async_computation.7 | async-start | bytes 2097152 | tf_op jit(solution)/shard_map/all_to_all | solution.py:258
  318.3 4.1 %copy.163 = bf16[128,8192]{1,0:T(8,128)(2,1)} copy(bf16[128,8192]{0,1:T(8,128)(2,1)} %bitcast.54) | data formatting | bytes 4194304
  322.4 4.1 %copy.164 = bf16[128,8192]{1,0:T(8,128)(2,1)} copy(bf16[128,8192]{0,1:T(8,128)(2,1)} %bitcast.74) | data formatting | bytes 4194304
  326.4 6.9 %all-to-all-done.7 = bf16[16,128,1,256]{1,3,2,0:T(8,128)(2,1)S(1)} async-done(((bf16[16,128,1,256]{1,3,2,0:T(8,128)(2,1)}), bf16[16,128,1,256]{1,3,2,0:T(8,128)(2,1)S(1)}, u32[]{:S(2)}, u32[]{:S(2)}) %all-to-all-start.7) | async-done | bytes 1048608 | tf_op jit(solution)/shard_map/all_to_all | solution.py:258
  334.2 2.1 reduce_sum.62
  (105 shorter events, 34.1 us)
Async XLA Ops:
  4.3 7.7 %copy-start.15 = (bf16[128,8192]{1,0:T(8,128)(2,1)S(1)}, bf16[128,8192]{1,0:T(8,128)(2,1)}, u32[]{:S(2)}) copy-start(bf16[128,8192]{1,0:T(8,128)(2,1)} %param.15) | copy-start | bytes 6291460
  4.3 23.2 %all-to-all-start.1 = ((bf16[128,16,256]{0,2,1:T(8,128)(2,1)}), bf16[128,16,256]{0,2,1:T(8,128)(2,1)S(1)}, u32[]{:S(2)}, u32[]{:S(2)}) async-start(bf16[128,16,256]{0,2,1:T(8,128)(2,1)} %bitcast.8), calls=%async_computation.1 | async-start | bytes 2097152 | tf_op jit(solution)/shard_map/all_to_all | solution.py:73
  27.5 4.7 %copy-start.17 = (s32[256,1]{0,1:T(1,128)S(1)}, s32[256,1]{0,1:T(1,128)}, u32[]{:S(2)}) copy-start(s32[256,1]{0,1:T(1,128)} %param.16) | copy-start | bytes 3076
  27.5 29.4 %all-to-all-start.4 = ((bf16[128,16,512]{0,2,1:T(8,128)(2,1)}), bf16[128,16,512]{0,2,1:T(8,128)(2,1)S(1)}, u32[]{:S(2)}, u32[]{:S(2)}) async-start(bf16[128,16,512]{0,2,1:T(8,128)(2,1)} %bitcast.221), calls=%async_computation.4 | async-start | bytes 4194304 | tf_op jit(solution)/shard_map/all_to_all | solution.py:182
  57.0 1.3 copy-start.8
  58.3 31.4 %all-to-all-start = ((bf16[128,16,512]{0,2,1:T(8,128)(2,1)}), bf16[128,16,512]{0,2,1:T(8,128)(2,1)}, u32[]{:S(2)}, u32[]{:S(2)}) async-start(bf16[128,16,512]{0,2,1:T(8,128)(2,1)} %bitcast.222), calls=%async_computation | async-start | bytes 4194304 | tf_op jit(solution)/shard_map/all_to_all | solution.py:72
  89.7 15.7 %copy-start.16 = (s32[16,64]{1,0:T(8,128)S(1)}, s32[16,64]{1,0:T(8,128)}, u32[]{:S(2)}) copy-start(s32[16,64]{1,0:T(8,128)} %param.17) | copy-start | bytes 12292
  89.7 64.2 %all-to-all-start.2 = ((bf16[16,2,1,2,128,128]{5,4,3,1,2,0:T(8,128)(2,1)}), bf16[16,2,1,2,128,128]{5,4,3,1,2,0:T(8,128)(2,1)}, u32[]{:S(2)}, u32[]{:S(2)}) async-start(bf16[16,2,1,2,128,128]{5,4,3,1,2,0:T(8,128)(2,1)} %bitcast.32), calls=%async_computation.2 | async-start | bytes 4194304 | tf_op jit(solution)/shard_map/all_to_all | solution.py:127
  105.0 3.6 %copy-start.9 = (bf16[128,16,512]{0,2,1:T(8,128)(2,1)S(1)}, bf16[128,16,512]{0,2,1:T(8,128)(2,1)}, u32[]{:S(2)}) copy-start(bf16[128,16,512]{0,2,1:T(8,128)(2,1)} %copy-done.8) | copy-start | bytes 6291460
  125.8 31.3 %copy-start.11 = (bf16[16,2,128,128]{3,2,1,0:T(8,128)(2,1)S(1)}, bf16[16,2,128,128]{3,2,1,0:T(8,128)(2,1)}, u32[]{:S(2)}) copy-start(bf16[16,2,128,128]{3,2,1,0:T(8,128)(2,1)} %gather_fusion.1) | copy-start | bytes 3145732
  157.1 1.6 copy-start.12
  159.0 2.0 copy-start.5
  159.1 20.0 %copy-start.14 = (bf16[16,2,1,1,128,128]{5,4,1,0,3,2:T(8,128)(2,1)}, bf16[16,2,1,1,128,128]{5,4,1,0,3,2:T(8,128)(2,1)S(1)}, u32[]{:S(2)}) copy-start(bf16[16,2,1,1,128,128]{5,4,1,0,3,2:T(8,128)(2,1)S(1)} %copy.142) | copy-start | bytes 3145732
  175.9 3.2 copy-start.7
  179.1 2.0 copy-start
  189.8 33.7 %all-to-all-start.3 = ((bf16[16,128,1,512]{1,3,2,0:T(8,128)(2,1)}), bf16[16,128,1,512]{1,3,2,0:T(8,128)(2,1)}, u32[]{:S(2)}, u32[]{:S(2)}) async-start(bf16[16,128,1,512]{1,3,2,0:T(8,128)(2,1)} %bitcast.224), calls=%async_computation.3 | async-start | bytes 4194304 | tf_op jit(solution)/shard_map/all_to_all | solution.py:179
  194.3 6.0 %copy-start.1 = (bf16[16,4,128,256]{3,2,1,0:T(8,128)(2,1)S(1)}, bf16[16,4,128,256]{3,2,1,0:T(8,128)(2,1)}, u32[]{:S(2)}) copy-start(bf16[16,4,128,256]{3,2,1,0:T(8,128)(2,1)} %copy-done) | copy-start | bytes 12582916
  200.3 2.1 copy-start.2
  200.3 3.1 copy-start.6
  205.4 1.9 copy-start.3
  223.5 55.8 %all-to-all-start.6 = ((bf16[16,2,1,2,128,128]{5,4,3,1,2,0:T(8,128)(2,1)}), bf16[16,2,1,2,128,128]{5,4,3,1,2,0:T(8,128)(2,1)}, u32[]{:S(2)}, u32[]{:S(2)}) async-start(bf16[16,2,1,2,128,128]{5,4,3,1,2,0:T(8,128)(2,1)} %bitcast.90), calls=%async_computation.6 | async-start | bytes 4194304 | tf_op jit(solution)/shard_map/all_to_all | solution.py:234
  279.3 34.0 %all-to-all-start.5 = ((bf16[16,128,1,512]{1,3,2,0:T(8,128)(2,1)}), bf16[16,128,1,512]{1,3,2,0:T(8,128)(2,1)}, u32[]{:S(2)}, u32[]{:S(2)}) async-start(bf16[16,128,1,512]{1,3,2,0:T(8,128)(2,1)} %bitcast.223), calls=%async_computation.5 | async-start | bytes 4194304 | tf_op jit(solution)/shard_map/all_to_all | solution.py:257
  284.0 2.2 copy-start.4
  286.2 1.6 slice-start
  293.4 1.6 copy-start.10
  293.4 1.8 copy-start.13
  313.3 20.1 %all-to-all-start.7 = ((bf16[16,128,1,256]{1,3,2,0:T(8,128)(2,1)}), bf16[16,128,1,256]{1,3,2,0:T(8,128)(2,1)S(1)}, u32[]{:S(2)}, u32[]{:S(2)}) async-start(bf16[16,128,1,256]{1,3,2,0:T(8,128)(2,1)} %bitcast.94), calls=%async_computation.7 | async-start | bytes 2097152 | tf_op jit(solution)/shard_map/all_to_all | solution.py:258
where the time goes:
time: 346 us; the launch traced here: 340 us
  waiting for transfers between devices  147 us (42%)
  local copies, waits for them, and re-layouts  72.4 us (21%)
  starting transfers between devices  54.2 us (16%)
  matrix products  39.2 us (11%)
  other arithmetic  25.5 us (7%)
    all_to_all x1, waiting for transfers between devices, local(): lax.all_to_all(returning, 'blk', split_axis=0, concat_axis=0, tiled=True)  39.3 us
    unnamed x45, local copies, waits for them, and re-layouts  31.7 us
    all_to_all x1, waiting for transfers between devices, local(): lax.all_to_all(outgoing, 'blk', split_axis=0, concat_axis=0, tiled=True)  28.1 us
    all_to_all x1, waiting for transfers between devices, local(): lax.all_to_all(query_split, 'sp', split_axis=1, concat_axis=0, tiled=True)  18.9 us
    all_to_all x1, waiting for transfers between devices, local(): lax.all_to_all(grad_split, 'sp', split_axis=1, concat_axis=0, tiled=True)  18.7 us
    all_to_all x1, starting transfers between devices, local(): lax.all_to_all(outgoing, 'blk', split_axis=0, concat_axis=0, tiled=True)  15.3 us
    all_to_all x1, waiting for transfers between devices, local(): lax.all_to_all(pair_split, 'sp', split_axis=1, concat_axis=0, tiled=True)  13.1 us
    all_to_all x1, waiting for transfers between devices, local(): lax.all_to_all(to_tokens(query_grad_heads), 'sp', split_axis=0, concat_ax...  11.4 us
  transfers between devices with their start and end apart: 8, of which 8 were waited for; matrix products, arithmetic and copies ran while one was open for 24% of the time, Pallas kernels for 0%

commit v1 on v0

v1 whole, which is shorter than its diff:
```python
import math

import jax
import jax.numpy as jnp
import numpy as np
from jax import lax
from jax.experimental import pallas as pl
from jax.experimental.pallas import tpu as pltpu
from jax.sharding import PartitionSpec as P

QUERY_HEAD_COUNT = 64
KEY_VALUE_HEADS = 8
HEAD_SIZE = 128
BLOCK = 128
CAP = 2
GROUP = QUERY_HEAD_COUNT // KEY_VALUE_HEADS
ROWS = GROUP * BLOCK
SLICES = 2 * KEY_VALUE_HEADS
MAX_CODE = 448.0
SCORE_SCALE = 1.0 / (HEAD_SIZE * math.sqrt(HEAD_SIZE))
BF16 = jnp.bfloat16
F32 = jnp.float32
VMEM_LIMIT = 48 * 1024 * 1024


def hadamard_table():
    index = np.arange(HEAD_SIZE)
    common = index[:, None] & index[None, :]
    parity = np.zeros_like(common)
    for bit in range(HEAD_SIZE.bit_length() - 1):
        parity += (common >> bit) & 1
    return np.where(parity % 2 == 0, 1.0, -1.0).astype(jnp.bfloat16)


def matmul(a, b):
    return lax.dot_general(a, b, (((1,), (0,)), ((), ())), preferred_element_type=F32)


def matmul_nt(a, b):
    return lax.dot_general(a, b, (((1,), (1,)), ((), ())), preferred_element_type=F32)


def matmul_tn(a, b):
    return lax.dot_general(a, b, (((0,), (0,)), ((), ())), preferred_element_type=F32)


def quantize(states, hadamard, inverse, factor):
    coded = jnp.clip(matmul(states, hadamard) * inverse, -MAX_CODE, MAX_CODE).astype(BF16)
    return (coded.astype(F32) * factor).astype(BF16)


def lanes(ref, head):
    return ref[:, head * HEAD_SIZE : (head + 1) * HEAD_SIZE]


def stack_heads(ref):
    return jnp.concatenate([lanes(ref, head) for head in range(GROUP)], axis=0)


def pack_kernel(factors, hadamard_ref, key_ref, value_ref, out_ref):
    hadamard = hadamard_ref[...]
    for head in range(KEY_VALUE_HEADS):
        out_ref[2 * head] = quantize(lanes(key_ref, head), hadamard, factors[0, head], factors[1, head])
        value = quantize(lanes(value_ref, head), hadamard, factors[2, head], factors[3, head])
        out_ref[2 * head + 1] = (matmul(value, hadamard) * (1.0 / HEAD_SIZE)).astype(BF16)


def pick_kernel(index, source_ref, out_ref):
    for slot in range(out_ref.shape[0]):
        out_ref[slot] = source_ref[index[slot]]


def pick_entries_kernel(index, own_ref, remote_ref, out_ref):
    count = own_ref.shape[0]
    for slot in range(out_ref.shape[0]):
        place = index[slot]

        @pl.when(place < count)
        def _():
            out_ref[slot] = own_ref[jnp.minimum(place, count - 1)]

        @pl.when(place >= count)
        def _():
            out_ref[slot] = remote_ref[jnp.maximum(place - count, 0)]


def accumulate_kernel(index, own_ref, remote_ref, out_ref, total):
    total[...] = jnp.zeros_like(total)
    count = own_ref.shape[0]
    for slot in range(count):
        place = index[slot]
        total[place] += own_ref[slot].astype(F32)
    for slot in range(remote_ref.shape[0]):
        place = index[count + slot]
        total[place] += remote_ref[slot].astype(F32)
    out_ref[...] = total[: out_ref.shape[0]].astype(BF16)


def finish_kernel(own_ref, listed_ref, key_ref, value_ref):
    for head in range(KEY_VALUE_HEADS):
        cols = slice(head * HEAD_SIZE, (head + 1) * HEAD_SIZE)
        total = own_ref[2 * head : 2 * head + 2] + listed_ref[2 * head : 2 * head + 2].astype(F32)
        key_ref[:, cols] = total[0].astype(BF16)
        value_ref[:, cols] = total[1].astype(BF16)


def causal_mask():
    keys = lax.broadcasted_iota(jnp.int32, (BLOCK, ROWS), 0)
    queries = lax.broadcasted_iota(jnp.int32, (BLOCK, ROWS), 1) % BLOCK
    return keys <= queries


def own_kernel(factors, hadamard_ref, query_ref, grad_ref, pair_ref, deq_ref, stats_ref):
    group = pl.program_id(0)
    hadamard = hadamard_ref[...]
    for head in range(GROUP):
        place = group * GROUP + head
        deq_ref[0, head * BLOCK : (head + 1) * BLOCK, :] = quantize(
            lanes(query_ref, head), hadamard, factors[0, place], factors[1, place]
        )
    scores = matmul_nt(pair_ref[0], deq_ref[0]) * SCORE_SCALE
    scores = jnp.where(causal_mask(), scores, -jnp.inf)
    top = jnp.max(scores, axis=0, keepdims=True)
    weights = jnp.exp(scores - top)
    prob_grad = matmul_nt(pair_ref[1], stack_heads(grad_ref))
    stats_ref[0, 0:1, :] = top
    stats_ref[0, 1:2, :] = jnp.sum(weights, axis=0, keepdims=True)
    stats_ref[0, 2:3, :] = jnp.sum(weights * prob_grad, axis=0, keepdims=True)


def listed_kernel(
    valid, hadamard_ref, deq_ref, grad_ref, pair_ref, stats_ref, pair_out, final_ref
):
    deq = deq_ref[0]
    grad = stack_heads(grad_ref)
    scores = matmul_nt(pair_ref[0], deq) * SCORE_SCALE
    scores = jnp.where(valid[0] > 0, scores, -jnp.inf)
    own_top = stats_ref[0, 0:1, :]
    top = jnp.maximum(own_top, jnp.max(scores, axis=0, keepdims=True))
    weights = jnp.exp(scores - top)
    shrink = jnp.exp(own_top - top)
    inverse = 1.0 / (stats_ref[0, 1:2, :] * shrink + jnp.sum(weights, axis=0, keepdims=True))
    prob_grad = matmul_nt(pair_ref[1], grad)
    delta = stats_ref[0, 2:3, :] * shrink + jnp.sum(weights * prob_grad, axis=0, keepdims=True)
    delta = delta * inverse
    probs = weights * inverse
    score_grad = (probs * (prob_grad - delta) * SCORE_SCALE).astype(BF16)
    key_sum = matmul(score_grad, deq).astype(BF16)
    pair_out[0] = matmul(key_sum, hadamard_ref[...]).astype(BF16)
    pair_out[1] = matmul(probs.astype(BF16), grad).astype(BF16)
    final_ref[0, 0:1, :] = top
    final_ref[0, 1:2, :] = inverse
    final_ref[0, 2:3, :] = delta


def finish_rows(array, out_ref):
    for head in range(GROUP):
        cols = slice(head * HEAD_SIZE, (head + 1) * HEAD_SIZE)
        out_ref[:, cols] = array[head * BLOCK : (head + 1) * BLOCK].astype(BF16)


def rest_kernel(
    valid,
    hadamard_ref,
    deq_ref,
    grad_ref,
    own_ref,
    listed_ref,
    final_ref,
    attention_ref,
    query_grad_ref,
    pair_out,
):
    hadamard = hadamard_ref[...]
    deq = deq_ref[0]
    grad = stack_heads(grad_ref)
    top = final_ref[0, 0:1, :]
    inverse = final_ref[0, 1:2, :]
    delta = final_ref[0, 2:3, :]

    def part(key, value, mask):
        scores = matmul_nt(key, deq) * SCORE_SCALE
        probs = jnp.exp(jnp.where(mask, scores, -jnp.inf) - top) * inverse
        prob_grad = matmul_nt(value, grad)
        score_grad = (probs * (prob_grad - delta) * SCORE_SCALE).astype(BF16)
        return probs.astype(BF16), score_grad

    own_probs, own_score = part(own_ref[0], own_ref[1], causal_mask())
    listed_probs, listed_score = part(listed_ref[0], listed_ref[1], valid[0] > 0)
    pair_out[0] = matmul(matmul(own_score, deq).astype(BF16), hadamard)
    pair_out[1] = matmul(own_probs, grad)
    keys = jnp.concatenate([own_ref[0], listed_ref[0]], axis=0)
    keys = matmul(keys, hadamard).astype(BF16)
    values = jnp.concatenate([own_ref[1], listed_ref[1]], axis=0)
    finish_rows(matmul_tn(jnp.concatenate([own_probs, listed_probs], axis=0), values), attention_ref)
    finish_rows(matmul_tn(jnp.concatenate([own_score, listed_score], axis=0), keys), query_grad_ref)


def params():
    return pltpu.CompilerParams(vmem_limit_bytes=VMEM_LIMIT)


def smem():
    return pl.BlockSpec(memory_space=pltpu.SMEM)


def vmem():
    return pl.BlockSpec(memory_space=pltpu.VMEM)


def shape(*dims, dtype=BF16):
    return jax.ShapeDtypeStruct(dims, dtype)


def pick(index, source):
    count = index.shape[0]
    return pl.pallas_call(
        pick_kernel,
        out_shape=shape(count, *source.shape[1:]),
        in_specs=[smem(), vmem()],
        out_specs=vmem(),
        compiler_params=params(),
        name="pick",
    )(index, source)


def pick_entries(index, own, remote):
    count = index.shape[0]
    return pl.pallas_call(
        pick_entries_kernel,
        out_shape=shape(count, *own.shape[1:]),
        in_specs=[smem(), vmem(), vmem()],
        out_specs=vmem(),
        compiler_params=params(),
        name="pick_entries",
    )(index, own, remote)


def accumulate(index, own, remote):
    return pl.pallas_call(
        accumulate_kernel,
        out_shape=shape(*own.shape),
        in_specs=[smem(), vmem(), vmem()],
        out_specs=vmem(),
        scratch_shapes=[pltpu.VMEM((own.shape[0] + 1, *own.shape[1:]), F32)],
        compiler_params=params(),
        name="accumulate",
    )(index, own, remote)


def pack(factors, hadamard, keys, values):
    return pl.pallas_call(
        pack_kernel,
        out_shape=shape(SLICES, BLOCK, HEAD_SIZE),
        in_specs=[smem(), vmem(), vmem(), vmem()],
        out_specs=vmem(),
        compiler_params=params(),
        name="pack",
    )(factors, hadamard, keys, values)


def finish(own, listed):
    out = shape(BLOCK, KEY_VALUE_HEADS * HEAD_SIZE)
    return pl.pallas_call(
        finish_kernel,
        out_shape=(out, out),
        in_specs=[vmem(), vmem()],
        out_specs=(vmem(), vmem()),
        compiler_params=params(),
        name="finish",
    )(own, listed)


HADAMARD = pl.BlockSpec((HEAD_SIZE, HEAD_SIZE), lambda m: (0, 0))
TOKENS = pl.BlockSpec((BLOCK, ROWS), lambda m: (0, m))
STACKED = pl.BlockSpec((1, ROWS, HEAD_SIZE), lambda m: (m, 0, 0))
PAIR = pl.BlockSpec((2, BLOCK, HEAD_SIZE), lambda m: (m, 0, 0))
STATS = pl.BlockSpec((1, 8, ROWS), lambda m: (m, 0, 0))
STATS_SHAPE = shape(KEY_VALUE_HEADS, 8, ROWS, dtype=F32)
UNIT = 2 * BLOCK * ROWS * HEAD_SIZE * KEY_VALUE_HEADS


def cost(units, megabytes):
    return pl.CostEstimate(
        flops=units * UNIT, bytes_accessed=megabytes << 20, transcendentals=BLOCK * ROWS * KEY_VALUE_HEADS
    )


def own_part(factors, hadamard, queries, cotangent, packed):
    return pl.pallas_call(
        own_kernel,
        grid=(KEY_VALUE_HEADS,),
        out_shape=(shape(KEY_VALUE_HEADS, ROWS, HEAD_SIZE), STATS_SHAPE),
        in_specs=[smem(), HADAMARD, TOKENS, TOKENS, PAIR],
        out_specs=(STACKED, STATS),
        compiler_params=params(),
        cost_estimate=cost(3, 7),
        name="own_part",
    )(factors, hadamard, queries, cotangent, packed)


def listed_part(valid, hadamard, deq, cotangent, listed, stats):
    return pl.pallas_call(
        listed_kernel,
        grid=(KEY_VALUE_HEADS,),
        out_shape=(shape(SLICES, BLOCK, HEAD_SIZE), STATS_SHAPE),
        in_specs=[smem(), HADAMARD, STACKED, TOKENS, PAIR, STATS],
        out_specs=(PAIR, STATS),
        compiler_params=params(),
        cost_estimate=cost(4, 6),
        name="listed_part",
    )(valid, hadamard, deq, cotangent, listed, stats)


def rest_part(valid, hadamard, deq, cotangent, packed, listed, final):
    rows = shape(BLOCK, QUERY_HEAD_COUNT * HEAD_SIZE)
    sums = shape(SLICES, BLOCK, HEAD_SIZE, dtype=F32)
    return pl.pallas_call(
        rest_kernel,
        grid=(KEY_VALUE_HEADS,),
        out_shape=(rows, rows, sums),
        in_specs=[smem(), HADAMARD, STACKED, TOKENS, PAIR, PAIR, STATS],
        out_specs=(TOKENS, TOKENS, PAIR),
        compiler_params=params(),
        cost_estimate=cost(10, 11),
        name="rest_part",
    )(valid, hadamard, deq, cotangent, packed, listed, final)


def exchange(array, axis):
    return lax.all_to_all(array, axis, split_axis=0, concat_axis=0, tiled=True)


def powers(exponent):
    up = (jnp.left_shift(1, exponent + 5)).astype(F32) * (1.0 / 32.0)
    down = (jnp.left_shift(1, 1 - exponent)).astype(F32) * 0.5
    return down, up


def local(
    queries,
    key_state_rows,
    value_state_rows,
    cotangent,
    block_list,
    query_exponent,
    key_block_exponent,
    value_block_exponent,
):
    sp_count = lax.axis_size("sp")
    blk_count = lax.axis_size("blk")
    sp_index = lax.axis_index("sp")
    blk_index = lax.axis_index("blk")
    hadamard = jnp.asarray(hadamard_table())

    def own_row(table):
        return lax.dynamic_index_in_dim(table, sp_index, 0, keepdims=False)

    query_factors = jnp.stack(powers(own_row(query_exponent)))
    pair_factors = jnp.stack(
        powers(own_row(key_block_exponent)) + powers(own_row(value_block_exponent))
    )

    listed = block_list.reshape(blk_count, sp_count)
    owners = listed // sp_count
    slots = jnp.arange(sp_count, dtype=jnp.int32)
    caps = jnp.arange(CAP, dtype=jnp.int32)
    groups = jnp.arange(blk_count, dtype=jnp.int32)
    remote = owners != groups[:, None]
    before = (
        (owners[:, :, None] == owners[:, None, :])
        & remote[:, None, :]
        & (slots[None, None, :] < slots[None, :, None])
    )
    rank = jnp.minimum(jnp.sum(before.astype(jnp.int32), axis=2), CAP - 1)
    serves = (
        remote[:, None, :]
        & (owners[:, None, :] == blk_index)
        & (rank[:, None, :] == caps[None, :, None])
    )
    serve_any = jnp.any(serves, axis=2).reshape(-1)
    serve_block = jnp.sum(jnp.where(serves, listed[:, None, :] % sp_count, 0), axis=2).reshape(-1)
    serve_block = jnp.clip(serve_block, 0, sp_count - 1)
    serve_target = jnp.where(serve_any, serve_block, sp_count)

    def own_group(table):
        return lax.dynamic_index_in_dim(table, blk_index, 0, keepdims=False)

    my_listed, my_owner, my_rank, my_remote = (
        own_group(listed),
        own_group(owners),
        own_group(rank),
        own_group(remote),
    )
    my_place = my_listed % sp_count
    entry_place = jnp.where(my_remote, sp_count + my_owner * CAP + my_rank, my_place)
    back = (
        my_remote[None, None, :]
        & (my_owner[None, None, :] == groups[:, None, None])
        & (my_rank[None, None, :] == caps[None, :, None])
    )
    back_entry = jnp.sum(jnp.where(back, slots[None, None, :], 0), axis=2).reshape(-1)
    back_entry = jnp.clip(back_entry, 0, sp_count - 1)
    entry_target = jnp.where(my_remote, sp_count, my_place)
    targets = jnp.concatenate([entry_target, serve_target])
    own_block = blk_index * sp_count + sp_index
    valid = (own_row(my_listed) != own_block).astype(jnp.int32).reshape(1)

    packed = pack(pair_factors, hadamard, key_state_rows, value_state_rows)
    slices = exchange(packed, "sp")
    outgoing, own_pairs = lax.optimization_barrier((pick(serve_block, slices), packed))
    arrived = exchange(outgoing.reshape(blk_count, CAP, BLOCK, HEAD_SIZE), "blk")
    arrived = arrived.reshape(blk_count * CAP, BLOCK, HEAD_SIZE)
    own = own_part(query_factors, hadamard, queries, cotangent, own_pairs)
    arrived, deq, stats = lax.optimization_barrier((arrived, *own))
    entries = exchange(pick_entries(entry_place, slices, arrived), "sp")
    entry_pairs, final = listed_part(valid, hadamard, deq, cotangent, entries, stats)
    entry_grads = exchange(entry_pairs, "sp")
    returning, final = lax.optimization_barrier((pick(back_entry, entry_grads), final))
    returned = exchange(returning.reshape(blk_count, CAP, BLOCK, HEAD_SIZE), "blk")
    returned = returned.reshape(blk_count * CAP, BLOCK, HEAD_SIZE)
    rest = rest_part(valid, hadamard, deq, cotangent, packed, entries, final)
    returned, attention, query_grad, own_sums = lax.optimization_barrier((returned, *rest))
    sums = exchange(accumulate(targets, entry_grads, returned), "sp")
    key_grad, value_grad = finish(own_sums, sums)
    return attention, query_grad, key_grad, value_grad


def solution(mesh):
    rows = P(("blk", "sp"), None)
    return jax.shard_map(
        local,
        mesh=mesh,
        in_specs=(rows, rows, rows, rows, P(), P("blk", None), P("blk", None), P("blk", None)),
        out_specs=(rows, rows, rows, rows),
        check_vma=False,
    )
```

time: 346 us -> 157 us (0.45); the launches traced: 340 us -> 156 us
  waiting for transfers between devices: 147 us -> 60.6 us
  local copies, waits for them, and re-layouts: 72.4 us -> 10.8 us
  matrix products: 39.2 us -> 0 us
  Pallas kernels: 0 us -> 35.3 us
  starting transfers between devices: 54.2 us -> 31.1 us
  other arithmetic: 25.5 us -> 2.45 us
  blocking collectives: 0 us -> 14.4 us
    all_to_all x8 -> x5, waiting for transfers between devices: 147 us -> 60.6 us  [exchange(): return lax.all_to_all(array, axis, split_axis=0, concat_axis=0, tiled=True)]
    dot_general x14 -> x0, matrix products: 39.2 us -> none  [the longest x1 5.98 us: local(): jnp.einsum('bmgqd,bmkd->bmgqk', grad_rot, value_part, preferred_element_t...]
    pallas_call x0 -> x9, Pallas kernels: none -> 35.3 us  [the longest x1 11.1 us: rest_part(): pl.pallas_call(rest_kernel, grid=(KEY_VALUE_HEADS,), out_shape=(rows, row...]
    all_to_all x8 -> x5, starting transfers between devices: 54.2 us -> 31.1 us  [exchange(): return lax.all_to_all(array, axis, split_axis=0, concat_axis=0, tiled=True)]
    unnamed x45 -> x27, local copies, waits for them, and re-layouts: 31.7 us -> 8.83 us
    reshape x11 -> x2, local copies, waits for them, and re-layouts: 17.5 us -> 0.18 us  [the longest x1 0.1 us: local(): serve_any = jnp.any(serves, axis=2).reshape(-1)]
    all_to_all x0 -> x1, blocking collectives: none -> 14.4 us  [exchange(): return lax.all_to_all(array, axis, split_axis=0, concat_axis=0, tiled=True)]
    sub x1 -> x0, other arithmetic: 10.2 us -> none  [local(): weights = jnp.exp(masked - row_max)]
  transfers between devices with their start and end apart: 8 -> 5, of which waited for: 8 -> 5; matrix products, arithmetic and copies ran while one was open for 24% -> 3% of each run, Pallas kernels for 0% -> 12%
where the time goes in v1:
time: 157 us; the launch traced here: 156 us
  waiting for transfers between devices  60.6 us (39%)
  Pallas kernels  35.3 us (22%)
  starting transfers between devices  31.1 us (20%)
  blocking collectives  14.4 us (9%)
  local copies, waits for them, and re-layouts  10.8 us (7%)
  other arithmetic  2.45 us (2%)
    all_to_all x5, waiting for transfers between devices, exchange(): return lax.all_to_all(array, axis, split_axis=0, concat_axis=0, tiled=True)  60.6 us
    all_to_all x5, starting transfers between devices, exchange(): return lax.all_to_all(array, axis, split_axis=0, concat_axis=0, tiled=True)  31.1 us
    all_to_all x1, blocking collectives, exchange(): return lax.all_to_all(array, axis, split_axis=0, concat_axis=0, tiled=True)  14.4 us
    pallas_call x1, Pallas kernels, rest_part(): pl.pallas_call(rest_kernel, grid=(KEY_VALUE_HEADS,), out_shape=(rows, row...  11.1 us
    unnamed x27, local copies, waits for them, and re-layouts  8.83 us
    pallas_call x1, Pallas kernels, listed_part(): pl.pallas_call(listed_kernel, grid=(KEY_VALUE_HEADS,), out_shape=(shape(S...  7.17 us
    pallas_call x1, Pallas kernels, own_part(): pl.pallas_call(own_kernel, grid=(KEY_VALUE_HEADS,), out_shape=(shape(KEY_...  6.92 us
    pallas_call x2, Pallas kernels, pick(): pl.pallas_call(pick_kernel, out_shape=shape(count, *source.shape[1:]), in...  3.17 us
  transfers between devices with their start and end apart: 5, of which 5 were waited for; matrix products, arithmetic and copies ran while one was open for 3% of the time, Pallas kernels for 12%

profile of v1, /device:TPU:1, one launch (start us, length us, event | category | flops | bytes accessed | tf_op | source)
XLA Modules:
  0.0 156.1 jit_solution(7223105232520807581)
XLA Ops:
  0.6 0.8 constant_dynamic-slice_fusion.2
  1.4 0.1 copy.23
  1.5 0.1 copy.22
  1.6 0.0 copy-start.7
  1.6 0.7 copy-done.7
  2.4 0.9 copy-done.9
  3.3 0.9 copy-done.10
  4.3 2.7 %pack.1.pair_ref.own_ref = bf16[16,128,128]{2,1,0:T(8,128)(2,1)} custom-call(f32[4,8]{1,0:T(4,128)S(1)} %pad_maximum_fusion.factors, bf16[128,128]{1,0:T(8,128)(2,1)S(1)} %copy-done.7, bf16[128,1024]{1,0:T(8,128)(2,1)S(1)} %copy-done.9, bf16[128,1024]{1,0:T(8,128)(2,1)S(1)} %copy-done.10), custom_call_target="tpu_custom_call" | custom-call | tf_op jit(solution)/shard_map/pack/pallas_call | solution.py:252
  6.9 7.6 %all-to-all-start = ((bf16[16,128,128]{2,1,0:T(8,128)(2,1)}), bf16[16,128,128]{2,1,0:T(8,128)(2,1)S(1)}, u32[]{:S(2)}, u32[]{:S(2)}) async-start(bf16[16,128,128]{2,1,0:T(8,128)(2,1)} %pack.1.pair_ref.own_ref), calls=%async_computation | async-start | bytes 1048576 | tf_op jit(solution)/shard_map/all_to_all | solution.py:331
  14.5 0.0 copy-start.8
  14.6 0.5 broadcast.270
  15.1 0.8 reduce.3
  15.8 0.1 reshape.245
  16.0 0.4 convert_reduce_fusion
  16.5 0.1 select_reduce_fusion.1
  16.6 0.1 select_reduce_fusion
  16.7 0.1 copy.18
  16.8 0.1 min.29.index
  16.9 7.9 %all-to-all-done.source_ref.own_ref = bf16[16,128,128]{2,1,0:T(8,128)(2,1)S(1)} async-done(((bf16[16,128,128]{2,1,0:T(8,128)(2,1)}), bf16[16,128,128]{2,1,0:T(8,128)(2,1)S(1)}, u32[]{:S(2)}, u32[]{:S(2)}) %all-to-all-start) | async-done | bytes 524320 | tf_op jit(solution)/shard_map/all_to_all | solution.py:331
  24.8 1.6 %pick.2 = bf16[32,128,128]{2,1,0:T(8,128)(2,1)} custom-call(s32[32]{0:T(128)S(1)} %min.29.index, bf16[16,128,128]{2,1,0:T(8,128)(2,1)S(1)} %all-to-all-done.source_ref.own_ref), custom_call_target="tpu_custom_call" | custom-call | tf_op jit(solution)/shard_map/pick/pallas_call | solution.py:217
  26.4 10.6 %all-to-all-start.1 = ((bf16[16,2,128,128]{3,2,1,0:T(8,128)(2,1)}), bf16[16,2,128,128]{3,2,1,0:T(8,128)(2,1)}, u32[]{:S(2)}, u32[]{:S(2)}) async-start(bf16[16,2,128,128]{3,2,1,0:T(8,128)(2,1)} %bitcast.5), calls=%async_computation.1 | async-start | bytes 2097152 | tf_op jit(solution)/shard_map/all_to_all | solution.py:331
  37.0 0.7 convert_multiply_fusion.1
  37.8 6.9 %own_part.1 = (bf16[8,1024,128]{2,1,0:T(8,128)(2,1)S(1)}, f32[8,8,1024]{2,1,0:T(8,128)S(1)}) custom-call(f32[2,64]{1,0:T(2,128)S(1)} %pad_maximum_fusion.1.factors, bf16[128,128]{1,0:T(8,128)(2,1)S(1)} %copy-done.8, bf16[128,8192]{1,0:T(8,128)(2,1)S(1)} %copy-done.1, bf16[128,8192]{1,0:T(8,128)(2,1)} %grad_ref.5, bf16[16,128,128]{2,1,0:T(8,128)(2,1)} %pack.1.pair_ref.own_ref), custom_call_target="tpu_custom_call" | custom-call | flops 805306368 | bytes 7340032 | tf_op jit(solution)/shard_map/own_part/pallas_call | solution.py:290
  44.7 1.3 copy-done.2
  46.0 19.1 %all-to-all-done.1 = bf16[16,2,128,128]{3,2,1,0:T(8,128)(2,1)} async-done(((bf16[16,2,128,128]{3,2,1,0:T(8,128)(2,1)}), bf16[16,2,128,128]{3,2,1,0:T(8,128)(2,1)}, u32[]{:S(2)}, u32[]{:S(2)}) %all-to-all-start.1) | async-done | bytes 1048608 | tf_op jit(solution)/shard_map/all_to_all | solution.py:331
  65.1 2.3 %pick_entries.1 = bf16[16,128,128]{2,1,0:T(8,128)(2,1)} custom-call(s32[16]{0:T(128)S(1)} %get-tuple-element.47.index, bf16[16,128,128]{2,1,0:T(8,128)(2,1)S(1)} %all-to-all-done.source_ref.own_ref, bf16[32,128,128]{2,1,0:T(8,128)(2,1)} %bitcast.6.remote_ref), custom_call_target="tpu_custom_call" | custom-call | tf_op jit(solution)/shard_map/pick_entries/pallas_call | solution.py:229
  67.3 3.6 %all-to-all-start.2 = ((bf16[16,128,128]{2,1,0:T(8,128)(2,1)}), bf16[16,128,128]{2,1,0:T(8,128)(2,1)S(1)}, u32[]{:S(2)}, u32[]{:S(2)}) async-start(bf16[16,128,128]{2,1,0:T(8,128)(2,1)} %pick_entries.1), calls=%async_computation.2 | async-start | bytes 1048576 | tf_op jit(solution)/shard_map/all_to_all | solution.py:331
  70.9 0.6 dynamic_slice.35
  72.2 9.8 %all-to-all-done.2.pair_ref.listed_ref = bf16[16,128,128]{2,1,0:T(8,128)(2,1)S(1)} async-done(((bf16[16,128,128]{2,1,0:T(8,128)(2,1)}), bf16[16,128,128]{2,1,0:T(8,128)(2,1)S(1)}, u32[]{:S(2)}, u32[]{:S(2)}) %all-to-all-start.2) | async-done | bytes 524320 | tf_op jit(solution)/shard_map/all_to_all | solution.py:331
  81.9 1.6 %copy-done.3 = bf16[8,1024,128]{2,1,0:T(8,128)(2,1)S(1)} copy-done((bf16[8,1024,128]{2,1,0:T(8,128)(2,1)S(1)}, bf16[8,1024,128]{2,1,0:T(8,128)(2,1)}, u32[]{:S(2)}) %copy-start.3) | copy-done | bytes 2097176
  83.5 7.2 %listed_part.1 = (bf16[16,128,128]{2,1,0:T(8,128)(2,1)}, f32[8,8,1024]{2,1,0:T(8,128)S(1)}) custom-call(s32[1]{0:T(128)} %bitcast.4.valid, bf16[128,128]{1,0:T(8,128)(2,1)S(1)} %copy-done.8, bf16[8,1024,128]{2,1,0:T(8,128)(2,1)S(1)} %copy-done.3, bf16[128,8192]{1,0:T(8,128)(2,1)S(1)} %copy-done, ...), custom_call_target="tpu_custom_call" | custom-call | flops 1073741824 | bytes 6291456 | tf_op jit(solution)/shard_map/listed_part/pallas_call | solution.py:303
  90.7 3.6 %all-to-all-start.3 = ((bf16[16,128,128]{2,1,0:T(8,128)(2,1)}), bf16[16,128,128]{2,1,0:T(8,128)(2,1)S(1)}, u32[]{:S(2)}, u32[]{:S(2)}) async-start(bf16[16,128,128]{2,1,0:T(8,128)(2,1)} %get-tuple-element.31), calls=%async_computation.3 | async-start | bytes 1048576 | tf_op jit(solution)/shard_map/all_to_all | solution.py:331
  94.3 0.1 copy.17
  94.4 0.1 min.27.index
  94.5 10.0 %all-to-all-done.3.source_ref.own_ref = bf16[16,128,128]{2,1,0:T(8,128)(2,1)S(1)} async-done(((bf16[16,128,128]{2,1,0:T(8,128)(2,1)}), bf16[16,128,128]{2,1,0:T(8,128)(2,1)S(1)}, u32[]{:S(2)}, u32[]{:S(2)}) %all-to-all-start.3) | async-done | bytes 524320 | tf_op jit(solution)/shard_map/all_to_all | solution.py:331
  104.4 1.6 %pick.3 = bf16[32,128,128]{2,1,0:T(8,128)(2,1)} custom-call(s32[32]{0:T(128)S(1)} %min.27.index, bf16[16,128,128]{2,1,0:T(8,128)(2,1)S(1)} %all-to-all-done.3.source_ref.own_ref), custom_call_target="tpu_custom_call" | custom-call | tf_op jit(solution)/shard_map/pick/pallas_call | solution.py:217
  106.0 5.7 %all-to-all-start.4 = ((bf16[16,2,128,128]{3,2,1,0:T(8,128)(2,1)}), bf16[16,2,128,128]{3,2,1,0:T(8,128)(2,1)S(1)}, u32[]{:S(2)}, u32[]{:S(2)}) async-start(bf16[16,2,128,128]{3,2,1,0:T(8,128)(2,1)} %bitcast.8), calls=%async_computation.4 | async-start | bytes 2097152 | tf_op jit(solution)/shard_map/all_to_all | solution.py:331
  111.7 0.1 fusion.1
  111.8 0.1 copy.21
  111.9 0.1 reshape.252
  112.1 0.1 pad_add_fusion.index
  112.1 1.6 %copy-done.4 = bf16[8,1024,128]{2,1,0:T(8,128)(2,1)S(1)} copy-done((bf16[8,1024,128]{2,1,0:T(8,128)(2,1)S(1)}, bf16[8,1024,128]{2,1,0:T(8,128)(2,1)}, u32[]{:S(2)}) %copy-start.4) | copy-done | bytes 2097176
  113.7 11.1 %rest_part.1 = (bf16[128,8192]{1,0:T(8,128)(2,1)}, bf16[128,8192]{1,0:T(8,128)(2,1)}, f32[16,128,128]{2,1,0:T(8,128)S(1)}) custom-call(s32[1]{0:T(128)} %bitcast.4.valid, bf16[128,128]{1,0:T(8,128)(2,1)S(1)} %copy-done.8, bf16[8,1024,128]{2,1,0:T(8,128)(2,1)S(1)} %copy-done.4, bf16[128,8192]{1,0:T(8,128)(2,1)} %grad_ref.5, ...), custom_call_target="tpu_custom_call" | custom-call | flops 2684354560 | bytes 11534336 | tf_op jit(solution)/shard_map/rest_part/pallas_call | solution.py:318
  124.9 1.0 copy-done.5
  125.8 13.9 %all-to-all-done.4 = bf16[16,2,128,128]{3,2,1,0:T(8,128)(2,1)S(1)} async-done(((bf16[16,2,128,128]{3,2,1,0:T(8,128)(2,1)}), bf16[16,2,128,128]{3,2,1,0:T(8,128)(2,1)S(1)}, u32[]{:S(2)}, u32[]{:S(2)}) %all-to-all-start.4) | async-done | bytes 1048608 | tf_op jit(solution)/shard_map/all_to_all | solution.py:331
  139.7 1.1 accumulate.1
  140.8 14.4 %all_to_all.30.listed_ref = bf16[16,128,128]{2,1,0:T(8,128)(2,1)S(1)} all-to-all(bf16[16,128,128]{2,1,0:T(8,128)(2,1)S(1)} %accumulate.1), channel_id=1, replica_groups=mesh['sp'=16,'blk'=16] {'sp'}, dimensions={0} | all-to-all | bytes 1048576 | tf_op jit(solution)/shard_map/all_to_all | solution.py:331
  155.1 0.9 finish.1
  (29 shorter events, 0.2 us)
Async XLA Ops:
  0.6 14.5 %copy-start.11 = (s32[256,1]{0,1:T(1,128)S(1)}, s32[256,1]{0,1:T(1,128)}, u32[]{:S(2)}) copy-start(s32[256,1]{0,1:T(1,128)} %param.13) | copy-start | bytes 3076
  1.6 0.8 copy-start.7
  2.4 0.9 copy-start.9
  3.3 0.9 copy-start.10
  6.9 17.9 %all-to-all-start = ((bf16[16,128,128]{2,1,0:T(8,128)(2,1)}), bf16[16,128,128]{2,1,0:T(8,128)(2,1)S(1)}, u32[]{:S(2)}, u32[]{:S(2)}) async-start(bf16[16,128,128]{2,1,0:T(8,128)(2,1)} %pack.1.pair_ref.own_ref), calls=%async_computation | async-start | bytes 1048576 | tf_op jit(solution)/shard_map/all_to_all | solution.py:331
  14.5 23.2 %copy-start.1 = (bf16[128,8192]{1,0:T(8,128)(2,1)S(1)}, bf16[128,8192]{1,0:T(8,128)(2,1)}, u32[]{:S(2)}) copy-start(bf16[128,8192]{1,0:T(8,128)(2,1)} %query_ref.1) | copy-start | bytes 6291460
  14.5 23.2 %copy-start.8 = (bf16[128,128]{1,0:T(8,128)(2,1)S(1)}, bf16[128,128]{1,0:T(8,128)(2,1)}, u32[]{:S(2)}) copy-start(bf16[128,128]{1,0:T(8,128)(2,1)} %constant.101.clone.hadamard_ref) | copy-start | bytes 98308
  26.4 38.7 %all-to-all-start.1 = ((bf16[16,2,128,128]{3,2,1,0:T(8,128)(2,1)}), bf16[16,2,128,128]{3,2,1,0:T(8,128)(2,1)}, u32[]{:S(2)}, u32[]{:S(2)}) async-start(bf16[16,2,128,128]{3,2,1,0:T(8,128)(2,1)} %bitcast.5), calls=%async_computation.1 | async-start | bytes 2097152 | tf_op jit(solution)/shard_map/all_to_all | solution.py:331
  44.7 1.3 copy-start.2
  46.0 35.9 %copy-start = (bf16[128,8192]{1,0:T(8,128)(2,1)S(1)}, bf16[128,8192]{1,0:T(8,128)(2,1)}, u32[]{:S(2)}) copy-start(bf16[128,8192]{1,0:T(8,128)(2,1)} %grad_ref.5) | copy-start | bytes 6291460
  67.3 14.6 %all-to-all-start.2 = ((bf16[16,128,128]{2,1,0:T(8,128)(2,1)}), bf16[16,128,128]{2,1,0:T(8,128)(2,1)S(1)}, u32[]{:S(2)}, u32[]{:S(2)}) async-start(bf16[16,128,128]{2,1,0:T(8,128)(2,1)} %pick_entries.1), calls=%async_computation.2 | async-start | bytes 1048576 | tf_op jit(solution)/shard_map/all_to_all | solution.py:331
  81.9 1.6 %copy-start.3 = (bf16[8,1024,128]{2,1,0:T(8,128)(2,1)S(1)}, bf16[8,1024,128]{2,1,0:T(8,128)(2,1)}, u32[]{:S(2)}) copy-start(bf16[8,1024,128]{2,1,0:T(8,128)(2,1)} %copy-done.2) | copy-start | bytes 6291460
  90.7 13.7 %all-to-all-start.3 = ((bf16[16,128,128]{2,1,0:T(8,128)(2,1)}), bf16[16,128,128]{2,1,0:T(8,128)(2,1)S(1)}, u32[]{:S(2)}, u32[]{:S(2)}) async-start(bf16[16,128,128]{2,1,0:T(8,128)(2,1)} %get-tuple-element.31), calls=%async_computation.3 | async-start | bytes 1048576 | tf_op jit(solution)/shard_map/all_to_all | solution.py:331
  106.0 33.7 %all-to-all-start.4 = ((bf16[16,2,128,128]{3,2,1,0:T(8,128)(2,1)}), bf16[16,2,128,128]{3,2,1,0:T(8,128)(2,1)S(1)}, u32[]{:S(2)}, u32[]{:S(2)}) async-start(bf16[16,2,128,128]{3,2,1,0:T(8,128)(2,1)} %bitcast.8), calls=%async_computation.4 | async-start | bytes 2097152 | tf_op jit(solution)/shard_map/all_to_all | solution.py:331
  112.1 1.6 %copy-start.4 = (bf16[8,1024,128]{2,1,0:T(8,128)(2,1)S(1)}, bf16[8,1024,128]{2,1,0:T(8,128)(2,1)}, u32[]{:S(2)}) copy-start(bf16[8,1024,128]{2,1,0:T(8,128)(2,1)} %copy-done.2) | copy-start | bytes 6291460
  124.9 1.0 copy-start.5
  139.7 15.4 %copy-start.6 = (f32[16,128,128]{2,1,0:T(8,128)S(1)}, f32[16,128,128]{2,1,0:T(8,128)}, u32[]{:S(2)}) copy-start(f32[16,128,128]{2,1,0:T(8,128)} %copy-done.5) | copy-start | bytes 3145732

commit v2 on v1

v2 whole, which is shorter than its diff:
```python
import math

import jax
import jax.numpy as jnp
import numpy as np
from jax import lax
from jax.experimental import pallas as pl
from jax.experimental.pallas import tpu as pltpu
from jax.sharding import PartitionSpec as P

QUERY_HEAD_COUNT = 64
KEY_VALUE_HEADS = 8
HEAD_SIZE = 128
BLOCK = 128
GROUP = QUERY_HEAD_COUNT // KEY_VALUE_HEADS
ROWS = GROUP * BLOCK
SLICES = 2 * KEY_VALUE_HEADS
PIECE = 8
MAX_CODE = 448.0
SCORE_SCALE = 1.0 / (HEAD_SIZE * math.sqrt(HEAD_SIZE))
BF16 = jnp.bfloat16
F32 = jnp.float32
CHUNK = 256
UNROLL = 16


def hadamard_table():
    index = np.arange(HEAD_SIZE)
    common = index[:, None] & index[None, :]
    parity = np.zeros_like(common)
    for bit in range(HEAD_SIZE.bit_length() - 1):
        parity += (common >> bit) & 1
    return np.where(parity % 2 == 0, 1.0, -1.0).astype(jnp.bfloat16)


def matmul(a, b):
    return lax.dot_general(a, b, (((1,), (0,)), ((), ())), preferred_element_type=F32)


def matmul_nt(a, b):
    return lax.dot_general(a, b, (((1,), (1,)), ((), ())), preferred_element_type=F32)


def matmul_tn(a, b):
    return lax.dot_general(a, b, (((0,), (0,)), ((), ())), preferred_element_type=F32)


def quantize(states, hadamard, inverse, factor):
    coded = jnp.clip(matmul(states, hadamard) * inverse, -MAX_CODE, MAX_CODE).astype(BF16)
    return (coded.astype(F32) * factor).astype(BF16)


def lanes(ref, head):
    return ref[:, head * HEAD_SIZE : (head + 1) * HEAD_SIZE]


def stack_heads(ref):
    return jnp.concatenate([lanes(ref, head) for head in range(GROUP)], axis=0)


def power(exponent, shift, scale):
    return jnp.left_shift(jnp.ones_like(exponent), exponent + shift).astype(F32) * scale


def own_powers(table, row):
    blocks = lax.broadcasted_iota(jnp.int32, table.shape, 1)
    level = jnp.sum(jnp.where(blocks == row, table, 0), axis=1, keepdims=True)
    return power(-level, 1, 0.5), power(level, 5, 1.0 / 32.0)


def pack_kernel(key_exponent, value_exponent, hadamard_ref, key_ref, value_ref, out_ref):
    hadamard = hadamard_ref[...]
    row = lax.axis_index("sp")

    def coded(ref, exponent_ref):
        stacked = jnp.concatenate([lanes(ref, head) for head in range(KEY_VALUE_HEADS)], axis=0)
        rotated = matmul(stacked, hadamard)
        down, up = own_powers(exponent_ref[...], row)
        parts = []
        for head in range(KEY_VALUE_HEADS):
            one = slice(head, head + 1)
            part = rotated[head * BLOCK : (head + 1) * BLOCK] * down[one, :]
            part = jnp.clip(part, -MAX_CODE, MAX_CODE).astype(BF16)
            parts.append((part.astype(F32) * up[one, :]).astype(BF16))
        return parts

    keys = coded(key_ref, key_exponent)
    values = matmul(jnp.concatenate(coded(value_ref, value_exponent), axis=0), hadamard)
    values = (values * (1.0 / HEAD_SIZE)).astype(BF16)
    for head in range(KEY_VALUE_HEADS):
        out_ref[2 * head] = keys[head]
        out_ref[2 * head + 1] = values[head * BLOCK : (head + 1) * BLOCK]


def pick_kernel(index, source_ref, out_ref):
    def some(step, carry):
        for place in range(UNROLL):
            row = step * UNROLL + place
            out_ref[row] = source_ref[index[row]]
        return carry

    lax.fori_loop(0, out_ref.shape[0] // UNROLL, some, 0)


def accumulate_kernel(index, part_ref, out_ref, even, odd):
    even[...] = jnp.zeros_like(even)
    odd[...] = jnp.zeros_like(odd)

    def some(step, carry):
        for place in range(UNROLL):
            row = step * UNROLL + place
            total = even if place % 2 == 0 else odd
            total[index[row]] += part_ref[row].astype(F32)
        return carry

    lax.fori_loop(0, part_ref.shape[0] // UNROLL, some, 0)
    out_ref[...] = (even[...] + odd[...]).astype(BF16)


def finish_kernel(own_ref, listed_ref, key_ref, value_ref):
    for head in range(KEY_VALUE_HEADS):
        cols = slice(head * HEAD_SIZE, (head + 1) * HEAD_SIZE)
        total = own_ref[2 * head : 2 * head + 2] + listed_ref[2 * head : 2 * head + 2].astype(F32)
        key_ref[:, cols] = total[0].astype(BF16)
        value_ref[:, cols] = total[1].astype(BF16)


def causal_mask():
    keys = lax.broadcasted_iota(jnp.int32, (BLOCK, ROWS), 0)
    queries = lax.broadcasted_iota(jnp.int32, (BLOCK, ROWS), 1) % BLOCK
    return keys <= queries


def own_kernel(exponent, hadamard_ref, query_ref, grad_ref, pair_ref, deq_ref, stats_ref):
    group = pl.program_id(0)
    hadamard = hadamard_ref[...]
    row = lax.axis_index("sp")
    for head in range(GROUP):
        level = exponent[row, group * GROUP + head]
        deq_ref[0, head * BLOCK : (head + 1) * BLOCK, :] = quantize(
            lanes(query_ref, head), hadamard, power(-level, 1, 0.5), power(level, 5, 1.0 / 32.0)
        )
    scores = matmul_nt(pair_ref[0], deq_ref[0]) * SCORE_SCALE
    scores = jnp.where(causal_mask(), scores, -jnp.inf)
    top = jnp.max(scores, axis=0, keepdims=True)
    weights = jnp.exp(scores - top)
    prob_grad = matmul_nt(pair_ref[1], stack_heads(grad_ref))
    stats_ref[0, 0:1, :] = top
    stats_ref[0, 1:2, :] = jnp.sum(weights, axis=0, keepdims=True)
    stats_ref[0, 2:3, :] = jnp.sum(weights * prob_grad, axis=0, keepdims=True)


def own_block():
    return lax.axis_index("blk") * lax.axis_size("sp") + lax.axis_index("sp")


def lists_other(index):
    block = own_block()
    return index[block] != block


def listed_kernel(
    index, hadamard_ref, deq_ref, grad_ref, pair_ref, stats_ref, pair_out, final_ref, score_scr, prob_scr
):
    listed = lists_other(index)

    def softmax(head, slot, start):
        cols = slice(start, start + CHUNK)
        grad = grad_rows(head, start // BLOCK, CHUNK // BLOCK)
        scores = matmul_nt(pair_ref[2 * head], deq_ref[head, cols, :])
        prob_grad = matmul_nt(pair_ref[2 * head + 1], grad)
        own_top = stats_ref[head, 0:1, cols]
        best = jnp.max(scores, axis=0, keepdims=True) * SCORE_SCALE
        top = jnp.maximum(own_top, jnp.where(listed, best, -jnp.inf))
        weights = jnp.exp(scores * SCORE_SCALE - jnp.where(listed, top, jnp.inf))
        shrink = jnp.exp(own_top - top)
        inverse = 1.0 / (
            stats_ref[head, 1:2, cols] * shrink + jnp.sum(weights, axis=0, keepdims=True)
        )
        delta = stats_ref[head, 2:3, cols] * shrink
        delta = (delta + jnp.sum(weights * prob_grad, axis=0, keepdims=True)) * inverse
        scaled = inverse * SCORE_SCALE
        prob_scr[slot, :, cols] = (weights * inverse).astype(BF16)
        score_scr[slot, :, cols] = (weights * (prob_grad * scaled - delta * scaled)).astype(BF16)
        final_ref[head, 0:1, cols] = top
        final_ref[head, 1:2, cols] = inverse
        final_ref[head, 2:3, cols] = delta

    def grad_rows(head, first, count):
        return jnp.concatenate(
            [lanes(grad_ref, head * GROUP + first + place) for place in range(count)], axis=0
        )

    for head in range(KEY_VALUE_HEADS + 1):
        if head < KEY_VALUE_HEADS:
            for start in range(0, ROWS, CHUNK):
                softmax(head, head % 2, start)
        if head > 0:
            last, slot = head - 1, (head - 1) % 2
            key_sum = matmul(score_scr[slot], deq_ref[last]).astype(BF16)
            pair_out[2 * last] = matmul(key_sum, hadamard_ref[...]).astype(BF16)
            value_sum = matmul(prob_scr[slot], grad_rows(last, 0, GROUP))
            pair_out[2 * last + 1] = value_sum.astype(BF16)


def finish_rows(array, out_ref):
    for head in range(GROUP):
        cols = slice(head * HEAD_SIZE, (head + 1) * HEAD_SIZE)
        out_ref[:, cols] = array[head * BLOCK : (head + 1) * BLOCK].astype(BF16)


def rest_kernel(
    index,
    hadamard_ref,
    deq_ref,
    grad_ref,
    own_ref,
    listed_ref,
    final_ref,
    attention_ref,
    query_grad_ref,
    pair_out,
):
    hadamard = hadamard_ref[...]
    deq = deq_ref[0]
    grad = stack_heads(grad_ref)
    top = final_ref[0, 0:1, :]
    inverse = final_ref[0, 1:2, :]
    delta = final_ref[0, 2:3, :]

    def part(key, value, mask):
        scores = matmul_nt(key, deq) * SCORE_SCALE
        probs = jnp.exp(jnp.where(mask, scores, -jnp.inf) - top) * inverse
        prob_grad = matmul_nt(value, grad)
        score_grad = (probs * (prob_grad - delta) * SCORE_SCALE).astype(BF16)
        return probs.astype(BF16), score_grad

    own_probs, own_score = part(own_ref[0], own_ref[1], causal_mask())
    listed_probs, listed_score = part(listed_ref[0], listed_ref[1], lists_other(index))
    pair_out[0] = matmul(matmul(own_score, deq).astype(BF16), hadamard)
    pair_out[1] = matmul(own_probs, grad)
    keys = jnp.concatenate([own_ref[0], listed_ref[0]], axis=0)
    keys = matmul(keys, hadamard).astype(BF16)
    values = jnp.concatenate([own_ref[1], listed_ref[1]], axis=0)
    finish_rows(matmul_tn(jnp.concatenate([own_probs, listed_probs], axis=0), values), attention_ref)
    finish_rows(matmul_tn(jnp.concatenate([own_score, listed_score], axis=0), keys), query_grad_ref)


def params(megabytes=16):
    return pltpu.CompilerParams(vmem_limit_bytes=megabytes << 20)


def smem():
    return pl.BlockSpec(memory_space=pltpu.SMEM)


def vmem():
    return pl.BlockSpec(memory_space=pltpu.VMEM)


def hbm():
    return pl.BlockSpec(memory_space=pltpu.HBM)


def shape(*dims, dtype=BF16):
    return jax.ShapeDtypeStruct(dims, dtype)


def pick(index, source):
    return pl.pallas_call(
        pick_kernel,
        out_shape=shape(*source.shape),
        in_specs=[smem(), vmem()],
        out_specs=vmem(),
        compiler_params=params(),
        name="pick",
    )(index, source)


def accumulate(index, parts):
    return pl.pallas_call(
        accumulate_kernel,
        out_shape=shape(*parts.shape),
        in_specs=[smem(), vmem()],
        out_specs=vmem(),
        scratch_shapes=[pltpu.VMEM(parts.shape, F32)] * 2,
        compiler_params=params(),
        name="accumulate",
    )(index, parts)


def pack(key_exponent, value_exponent, hadamard, keys, values):
    return pl.pallas_call(
        pack_kernel,
        out_shape=shape(SLICES, BLOCK, HEAD_SIZE),
        in_specs=[vmem()] * 5,
        out_specs=vmem(),
        compiler_params=params(60),
        name="pack",
    )(key_exponent, value_exponent, hadamard, keys, values)


def finish(own, listed):
    out = shape(BLOCK, KEY_VALUE_HEADS * HEAD_SIZE)
    return pl.pallas_call(
        finish_kernel,
        out_shape=(out, out),
        in_specs=[vmem(), vmem()],
        out_specs=(vmem(), vmem()),
        compiler_params=params(),
        name="finish",
    )(own, listed)


HADAMARD = pl.BlockSpec((HEAD_SIZE, HEAD_SIZE), lambda m: (0, 0))
TOKENS = pl.BlockSpec((BLOCK, ROWS), lambda m: (0, m))
STACKED = pl.BlockSpec((1, ROWS, HEAD_SIZE), lambda m: (m, 0, 0))
PAIR = pl.BlockSpec((2, BLOCK, HEAD_SIZE), lambda m: (m, 0, 0))
STATS = pl.BlockSpec((1, 8, ROWS), lambda m: (m, 0, 0))
STATS_SHAPE = shape(KEY_VALUE_HEADS, 8, ROWS, dtype=F32)
UNIT = 2 * BLOCK * ROWS * HEAD_SIZE * KEY_VALUE_HEADS


def cost(units, megabytes):
    return pl.CostEstimate(
        flops=units * UNIT, bytes_accessed=megabytes << 20, transcendentals=BLOCK * ROWS * KEY_VALUE_HEADS
    )


def own_part(exponent, hadamard, queries, cotangent, packed):
    return pl.pallas_call(
        own_kernel,
        grid=(KEY_VALUE_HEADS,),
        out_shape=(shape(KEY_VALUE_HEADS, ROWS, HEAD_SIZE), STATS_SHAPE),
        in_specs=[smem(), HADAMARD, TOKENS, TOKENS, PAIR],
        out_specs=(STACKED, STATS),
        compiler_params=params(),
        cost_estimate=cost(3, 7),
        name="own_part",
    )(exponent, hadamard, queries, cotangent, packed)


def listed_part(index, hadamard, deq, cotangent, listed, stats):
    return pl.pallas_call(
        listed_kernel,
        out_shape=(shape(SLICES, BLOCK, HEAD_SIZE), STATS_SHAPE),
        in_specs=[smem()] + [vmem()] * 5,
        out_specs=(vmem(), vmem()),
        scratch_shapes=[pltpu.VMEM((2, BLOCK, ROWS), BF16)] * 2,
        compiler_params=params(),
        cost_estimate=cost(4, 6),
        name="listed_part",
    )(index, hadamard, deq, cotangent, listed, stats)


def rest_part(index, hadamard, deq, cotangent, packed, listed, final):
    rows = shape(BLOCK, QUERY_HEAD_COUNT * HEAD_SIZE)
    sums = shape(SLICES, BLOCK, HEAD_SIZE, dtype=F32)
    return pl.pallas_call(
        rest_kernel,
        grid=(KEY_VALUE_HEADS,),
        out_shape=(rows, rows, sums),
        in_specs=[smem(), HADAMARD, STACKED, TOKENS, PAIR, PAIR, STATS],
        out_specs=(TOKENS, TOKENS, PAIR),
        compiler_params=params(),
        cost_estimate=cost(10, 11),
        name="rest_part",
    )(index, hadamard, deq, cotangent, packed, listed, final)


def exchange(array):
    pieces = array.reshape(-1, PIECE, HEAD_SIZE)
    return lax.all_to_all(pieces, ("blk", "sp"), split_axis=0, concat_axis=0, tiled=True)


def whole(pieces):
    return pieces.reshape(SLICES, BLOCK, HEAD_SIZE)


def local(
    queries,
    key_state_rows,
    value_state_rows,
    cotangent,
    block_list,
    query_exponent,
    key_block_exponent,
    value_block_exponent,
):
    hadamard = jnp.asarray(hadamard_table())
    index = block_list.reshape(-1)
    packed = pack(
        key_block_exponent.T, value_block_exponent.T, hadamard, key_state_rows, value_state_rows
    )
    pieces = exchange(packed)
    own = own_part(query_exponent, hadamard, queries, cotangent, packed)
    pieces, deq, stats = lax.optimization_barrier((pieces, *own))
    entries = whole(exchange(pick(index, pieces)))
    entry_pairs, final = listed_part(index, hadamard, deq, cotangent, entries, stats)
    parts = exchange(entry_pairs)
    rest = rest_part(index, hadamard, deq, cotangent, packed, entries, final)
    parts, attention, query_grad, own_sums = lax.optimization_barrier((parts, *rest))
    sums = whole(exchange(accumulate(index, parts)))
    key_grad, value_grad = finish(own_sums, sums)
    return attention, query_grad, key_grad, value_grad


def solution(mesh):
    rows = P(("blk", "sp"), None)
    return jax.shard_map(
        local,
        mesh=mesh,
        in_specs=(rows, rows, rows, rows, P(), P("blk", None), P("blk", None), P("blk", None)),
        out_specs=(rows, rows, rows, rows),
        check_vma=False,
    )
```

time: 157 us -> 129 us (0.82)
  waiting for transfers between devices: 60.6 us -> 17.5 us
  blocking collectives: 14.4 us -> 54 us
  starting transfers between devices: 31.1 us -> 21 us
  Pallas kernels: 35.3 us -> 26.7 us
  other arithmetic: 2.45 us -> 0 us
  local copies, waits for them, and re-layouts: 10.8 us -> 8.42 us
    all_to_all x5 -> x2, waiting for transfers between devices: 60.6 us -> 17.5 us  [exchange(): lax.all_to_all(pieces, ('blk', 'sp'), split_axis=0, concat_axis=0, tiled=...]
    all_to_all x1 -> x2, blocking collectives: 14.4 us -> 54 us  [exchange(): lax.all_to_all(pieces, ('blk', 'sp'), split_axis=0, concat_axis=0, tiled=...]
    all_to_all x5 -> x2, starting transfers between devices: 31.1 us -> 21 us  [exchange(): lax.all_to_all(pieces, ('blk', 'sp'), split_axis=0, concat_axis=0, tiled=...]
    pallas_call x5 -> x3, Pallas kernels: 13.7 us -> 6.8 us  [the longest x1 4.58 us: listed_part(): pl.pallas_call(listed_kernel, out_shape=(shape(SLICES, BLOCK, HEAD_SIZE),...]
    unnamed x27 -> x30, local copies, waits for them, and re-layouts: 8.83 us -> 8.42 us
  transfers between devices with their start and end apart: 5 -> 2, of which waited for: 5 -> 2; matrix products, arithmetic and copies ran while one was open for 3% -> 0% of each run, Pallas kernels for 12% -> 13%
where the time goes in v2:
time: 129 us; the launch traced here: 128 us
  blocking collectives  54 us (42%)
  Pallas kernels  26.7 us (21%)
  starting transfers between devices  21 us (16%)
  waiting for transfers between devices  17.5 us (14%)
  local copies, waits for them, and re-layouts  8.42 us (7%)
    all_to_all x2, blocking collectives, exchange(): lax.all_to_all(pieces, ('blk', 'sp'), split_axis=0, concat_axis=0, tiled=...  54 us
    all_to_all x2, starting transfers between devices, exchange(): lax.all_to_all(pieces, ('blk', 'sp'), split_axis=0, concat_axis=0, tiled=...  21 us
    all_to_all x2, waiting for transfers between devices, exchange(): lax.all_to_all(pieces, ('blk', 'sp'), split_axis=0, concat_axis=0, tiled=...  17.5 us
    pallas_call x1, Pallas kernels, rest_part(): pl.pallas_call(rest_kernel, grid=(KEY_VALUE_HEADS,), out_shape=(rows, row...  10.9 us
    unnamed x30, local copies, waits for them, and re-layouts  8.42 us
    pallas_call x1, Pallas kernels, own_part(): pl.pallas_call(own_kernel, grid=(KEY_VALUE_HEADS,), out_shape=(shape(KEY_...  5.57 us
    pallas_call x1, Pallas kernels, listed_part(): pl.pallas_call(listed_kernel, out_shape=(shape(SLICES, BLOCK, HEAD_SIZE),...  4.58 us
  transfers between devices with their start and end apart: 2, of which 2 were waited for; matrix products, arithmetic and copies ran while one was open for 0% of the time, Pallas kernels for 13%

profile of v2, /device:TPU:1, one launch (start us, length us, event | category | flops | bytes accessed | tf_op | source)
XLA Modules:
  0.0 128.4 jit_solution(18140271852409430930)
XLA Ops:
  0.6 0.0 copy-start.12
  0.6 0.0 copy-start
  0.7 0.0 copy-start.14
  0.7 2.5 %pack.1.pair_ref.own_ref = bf16[16,128,128]{2,1,0:T(8,128)(2,1)} custom-call(s32[8,16]{1,0:T(8,128)} %bitcast.16, s32[8,16]{1,0:T(8,128)} %bitcast.17, bf16[128,128]{1,0:T(8,128)(2,1)} %constant.2.clone.hadamard_ref, bf16[128,1024]{1,0:T(8,128)(2,1)} %key_ref.1, bf16[128,1024]{1,0:T(8,128)(2,1)} %value_ref.1), custom_call_target="tpu_custom_call" | custom-call | tf_op jit(solution)/shard_map/pack/pallas_call | solution.py:293
  3.2 15.7 %all-to-all-start = ((bf16[256,8,128]{2,1,0:T(8,128)(2,1)}), bf16[256,8,128]{2,1,0:T(8,128)(2,1)S(1)}, u32[]{:S(2)}, u32[]{:S(2)}) async-start(bf16[256,8,128]{2,1,0:T(8,128)(2,1)} %bitcast.7), calls=%async_computation | async-start | bytes 1048576 | tf_op jit(solution)/shard_map/all_to_all | solution.py:373
  18.8 0.0 copy-done.12
  18.8 0.0 copy-done
  18.8 0.0 copy-done.14
  18.8 0.0 copy-start.1
  18.9 1.1 copy-done.1
  19.9 0.0 copy-start.3
  19.9 1.6 %copy-done.3 = bf16[128,8192]{1,0:T(8,128)(2,1)S(1)} copy-done((bf16[128,8192]{1,0:T(8,128)(2,1)S(1)}, bf16[128,8192]{1,0:T(8,128)(2,1)}, u32[]{:S(2)}) %copy-start.3) | copy-done | bytes 2097176
  21.5 0.0 copy-start.13
  21.5 5.6 %own_part.1 = (bf16[8,1024,128]{2,1,0:T(8,128)(2,1)S(1)}, f32[8,8,1024]{2,1,0:T(8,128)S(1)}) custom-call(s32[16,64]{1,0:T(8,128)S(1)} %copy-done.14, bf16[128,128]{1,0:T(8,128)(2,1)S(1)} %copy-done.12, bf16[128,8192]{1,0:T(8,128)(2,1)S(1)} %copy-done.3, bf16[128,8192]{1,0:T(8,128)(2,1)S(1)} %copy-done, bf16[16,128,128]{2,1,0:T(8,128)(2,1)S(1)} %copy-done.1), custom_call_target="tpu_custom_call" | custom-call | flops 805306368 | bytes 7340032 | tf_op jit(solution)/shard_map/own_part/pallas_call | solution.py:331
  27.1 0.0 copy-start.4
  27.1 1.3 %copy-done.4 = bf16[8,1024,128]{2,1,0:T(8,128)(2,1)} copy-done((bf16[8,1024,128]{2,1,0:T(8,128)(2,1)}, bf16[8,1024,128]{2,1,0:T(8,128)(2,1)S(1)}, u32[]{:S(2)}) %copy-start.4) | copy-done | bytes 2097176
  28.4 11.2 %all-to-all-done.source_ref = bf16[256,8,128]{2,1,0:T(8,128)(2,1)S(1)} async-done(((bf16[256,8,128]{2,1,0:T(8,128)(2,1)}), bf16[256,8,128]{2,1,0:T(8,128)(2,1)S(1)}, u32[]{:S(2)}, u32[]{:S(2)}) %all-to-all-start) | async-done | bytes 524320 | tf_op jit(solution)/shard_map/all_to_all | solution.py:373
  39.6 0.0 copy-start.5
  39.6 0.0 copy-done.13
  39.7 0.9 pick.1
  40.6 26.0 %all_to_all.20 = bf16[256,8,128]{2,1,0:T(8,128)(2,1)S(1)} all-to-all(bf16[256,8,128]{2,1,0:T(8,128)(2,1)S(1)} %pick.1), channel_id=1, replica_groups=mesh['sp'=16,'blk'=16] {'blk','sp'}, dimensions={0} | all-to-all | bytes 1048576 | tf_op jit(solution)/shard_map/all_to_all | solution.py:373
  66.5 0.0 copy-start.7
  66.6 0.0 copy-done.5
  66.6 0.0 copy-start.2
  66.6 4.6 %listed_part.1 = (bf16[16,128,128]{2,1,0:T(8,128)(2,1)S(1)}, f32[8,8,1024]{2,1,0:T(8,128)S(1)}) custom-call(s32[256]{0:T(256)S(1)} %bitcast.13, bf16[128,128]{1,0:T(8,128)(2,1)S(1)} %copy-done.12, bf16[8,1024,128]{2,1,0:T(8,128)(2,1)S(1)} %copy-done.5, bf16[128,8192]{1,0:T(8,128)(2,1)S(1)} %copy-done, bf16[16,128,128]{2,1,0:T(8,128)(2,1)S(1)} %bitcast.9, ...), custom_call_target="tpu_custom_call" | custom-call | flops 1073741824 | bytes 6291456 | tf_op jit(solution)/shard_map/listed_part/pallas_call | solution.py:344
  71.1 0.0 copy-done.7
  71.2 0.0 copy-start.11
  71.2 0.8 copy-done.11
  71.9 5.4 %all-to-all-start.2 = ((bf16[256,8,128]{2,1,0:T(8,128)(2,1)}), bf16[256,8,128]{2,1,0:T(8,128)(2,1)S(1)}, u32[]{:S(2)}, u32[]{:S(2)}) async-start(bf16[256,8,128]{2,1,0:T(8,128)(2,1)} %bitcast.11), calls=%async_computation.2 | async-start | bytes 1048576 | tf_op jit(solution)/shard_map/all_to_all | solution.py:373
  77.3 0.0 copy-done.2
  77.3 0.0 copy-start.6
  77.3 1.6 %copy-done.6 = bf16[8,1024,128]{2,1,0:T(8,128)(2,1)S(1)} copy-done((bf16[8,1024,128]{2,1,0:T(8,128)(2,1)S(1)}, bf16[8,1024,128]{2,1,0:T(8,128)(2,1)}, u32[]{:S(2)}) %copy-start.6) | copy-done | bytes 2097176
  78.9 0.0 copy-start.8
  78.9 1.0 copy-done.8
  80.0 10.9 %rest_part.1 = (bf16[128,8192]{1,0:T(8,128)(2,1)}, bf16[128,8192]{1,0:T(8,128)(2,1)}, f32[16,128,128]{2,1,0:T(8,128)S(1)}) custom-call(s32[256]{0:T(256)S(1)} %bitcast.14, bf16[128,128]{1,0:T(8,128)(2,1)S(1)} %copy-done.12, bf16[8,1024,128]{2,1,0:T(8,128)(2,1)S(1)} %copy-done.6, bf16[128,8192]{1,0:T(8,128)(2,1)S(1)} %copy-done, ...), custom_call_target="tpu_custom_call" | custom-call | flops 2684354560 | bytes 11534336 | tf_op jit(solution)/shard_map/rest_part/pallas_call | solution.py:359
  90.8 0.0 copy-start.9
  90.8 1.0 copy-done.9
  91.8 6.3 %all-to-all-done.2.part_ref = bf16[256,8,128]{2,1,0:T(8,128)(2,1)S(1)} async-done(((bf16[256,8,128]{2,1,0:T(8,128)(2,1)}), bf16[256,8,128]{2,1,0:T(8,128)(2,1)S(1)}, u32[]{:S(2)}, u32[]{:S(2)}) %all-to-all-start.2) | async-done | bytes 524320 | tf_op jit(solution)/shard_map/all_to_all | solution.py:373
  98.1 0.0 copy-start.10
  98.1 1.3 %accumulate.1 = bf16[256,8,128]{2,1,0:T(8,128)(2,1)S(1)} custom-call(s32[256]{0:T(256)S(1)} %bitcast.15, bf16[256,8,128]{2,1,0:T(8,128)(2,1)S(1)} %all-to-all-done.2.part_ref), custom_call_target="tpu_custom_call" | custom-call | tf_op jit(solution)/shard_map/accumulate/pallas_call | solution.py:281
  99.5 28.0 %all_to_all.21 = bf16[256,8,128]{2,1,0:T(8,128)(2,1)S(1)} all-to-all(bf16[256,8,128]{2,1,0:T(8,128)(2,1)S(1)} %accumulate.1), channel_id=1, replica_groups=mesh['sp'=16,'blk'=16] {'blk','sp'}, dimensions={0} | all-to-all | bytes 1048576 | tf_op jit(solution)/shard_map/all_to_all | solution.py:373
  127.5 0.0 copy-done.10
  127.5 0.9 finish.1
Async XLA Ops:
  0.6 18.2 %copy-start.12 = (bf16[128,128]{1,0:T(8,128)(2,1)S(1)}, bf16[128,128]{1,0:T(8,128)(2,1)}, u32[]{:S(2)}) copy-start(bf16[128,128]{1,0:T(8,128)(2,1)} %constant.2.clone.hadamard_ref) | copy-start | bytes 98308
  0.6 18.2 %copy-start = (bf16[128,8192]{1,0:T(8,128)(2,1)S(1)}, bf16[128,8192]{1,0:T(8,128)(2,1)}, u32[]{:S(2)}) copy-start(bf16[128,8192]{1,0:T(8,128)(2,1)} %grad_ref.5) | copy-start | bytes 6291460
  0.7 18.2 %copy-start.14 = (s32[16,64]{1,0:T(8,128)S(1)}, s32[16,64]{1,0:T(8,128)}, u32[]{:S(2)}) copy-start(s32[16,64]{1,0:T(8,128)} %exponent.1) | copy-start | bytes 12292
  3.2 36.5 %all-to-all-start = ((bf16[256,8,128]{2,1,0:T(8,128)(2,1)}), bf16[256,8,128]{2,1,0:T(8,128)(2,1)S(1)}, u32[]{:S(2)}, u32[]{:S(2)}) async-start(bf16[256,8,128]{2,1,0:T(8,128)(2,1)} %bitcast.7), calls=%async_computation | async-start | bytes 1048576 | tf_op jit(solution)/shard_map/all_to_all | solution.py:373
  18.8 1.1 copy-start.1
  19.9 1.6 %copy-start.3 = (bf16[128,8192]{1,0:T(8,128)(2,1)S(1)}, bf16[128,8192]{1,0:T(8,128)(2,1)}, u32[]{:S(2)}) copy-start(bf16[128,8192]{1,0:T(8,128)(2,1)} %query_ref.1) | copy-start | bytes 6291460
  21.5 18.1 %copy-start.13 = (s32[256,1]{0,1:T(1,128)S(1)}, s32[256,1]{0,1:T(1,128)}, u32[]{:S(2)}) copy-start(s32[256,1]{0,1:T(1,128)} %param.13) | copy-start | bytes 3076
  27.1 1.3 %copy-start.4 = (bf16[8,1024,128]{2,1,0:T(8,128)(2,1)}, bf16[8,1024,128]{2,1,0:T(8,128)(2,1)S(1)}, u32[]{:S(2)}) copy-start(bf16[8,1024,128]{2,1,0:T(8,128)(2,1)S(1)} %get-tuple-element.22.deq_ref) | copy-start | bytes 6291460
  39.6 26.9 %copy-start.5 = (bf16[8,1024,128]{2,1,0:T(8,128)(2,1)S(1)}, bf16[8,1024,128]{2,1,0:T(8,128)(2,1)}, u32[]{:S(2)}) copy-start(bf16[8,1024,128]{2,1,0:T(8,128)(2,1)} %copy-done.4) | copy-start | bytes 6291460
  66.5 4.6 %copy-start.7 = (bf16[256,8,128]{2,1,0:T(8,128)(2,1)}, bf16[256,8,128]{2,1,0:T(8,128)(2,1)S(1)}, u32[]{:S(2)}) copy-start(bf16[256,8,128]{2,1,0:T(8,128)(2,1)S(1)} %all_to_all.20) | copy-start | bytes 1572868
  66.6 10.8 %copy-start.2 = (bf16[16,128,128]{2,1,0:T(8,128)(2,1)S(1)}, bf16[16,128,128]{2,1,0:T(8,128)(2,1)}, u32[]{:S(2)}) copy-start(bf16[16,128,128]{2,1,0:T(8,128)(2,1)} %pack.1.pair_ref.own_ref) | copy-start | bytes 1572868
  71.2 0.8 copy-start.11
  71.9 26.2 %all-to-all-start.2 = ((bf16[256,8,128]{2,1,0:T(8,128)(2,1)}), bf16[256,8,128]{2,1,0:T(8,128)(2,1)S(1)}, u32[]{:S(2)}, u32[]{:S(2)}) async-start(bf16[256,8,128]{2,1,0:T(8,128)(2,1)} %bitcast.11), calls=%async_computation.2 | async-start | bytes 1048576 | tf_op jit(solution)/shard_map/all_to_all | solution.py:373
  77.3 1.6 %copy-start.6 = (bf16[8,1024,128]{2,1,0:T(8,128)(2,1)S(1)}, bf16[8,1024,128]{2,1,0:T(8,128)(2,1)}, u32[]{:S(2)}) copy-start(bf16[8,1024,128]{2,1,0:T(8,128)(2,1)} %copy-done.4) | copy-start | bytes 6291460
  78.9 1.0 copy-start.8
  90.8 1.0 copy-start.9
  98.1 29.4 %copy-start.10 = (f32[16,128,128]{2,1,0:T(8,128)S(1)}, f32[16,128,128]{2,1,0:T(8,128)}, u32[]{:S(2)}) copy-start(f32[16,128,128]{2,1,0:T(8,128)} %copy-done.9) | copy-start | bytes 3145732

commit v3 on v2

--- a/solution.py
+++ b/solution.py
@@ -331,7 +331,7 @@
     return pl.pallas_call(
         own_kernel,
         grid=(KEY_VALUE_HEADS,),
-        out_shape=(shape(KEY_VALUE_HEADS, ROWS, HEAD_SIZE), STATS_SHAPE),
+        out_shape=(pltpu.HBM((KEY_VALUE_HEADS, ROWS, HEAD_SIZE), BF16), STATS_SHAPE),
         in_specs=[smem(), HADAMARD, TOKENS, TOKENS, PAIR],
         out_specs=(STACKED, STATS),
         compiler_params=params(),
@@ -355,7 +355,7 @@
 
 def rest_part(index, hadamard, deq, cotangent, packed, listed, final):
     rows = shape(BLOCK, QUERY_HEAD_COUNT * HEAD_SIZE)
-    sums = shape(SLICES, BLOCK, HEAD_SIZE, dtype=F32)
+    sums = pltpu.HBM((SLICES, BLOCK, HEAD_SIZE), F32)
     return pl.pallas_call(
         rest_kernel,
         grid=(KEY_VALUE_HEADS,),
@@ -398,7 +398,8 @@
     entries = whole(exchange(pick(index, pieces)))
     entry_pairs, final = listed_part(index, hadamard, deq, cotangent, entries, stats)
     parts = exchange(entry_pairs)
-    rest = rest_part(index, hadamard, deq, cotangent, packed, entries, final)
+    held = pltpu.with_memory_space_constraint(deq, pltpu.HBM)
+    rest = rest_part(index, hadamard, held, cotangent, packed, entries, final)
     parts, attention, query_grad, own_sums = lax.optimization_barrier((parts, *rest))
     sums = whole(exchange(accumulate(index, parts)))
     key_grad, value_grad = finish(own_sums, sums)

time: 129 us -> 127 us (0.984)
  local copies, waits for them, and re-layouts: 8.42 us -> 4.51 us
  waiting for transfers between devices: 17.5 us -> 20.5 us
  blocking collectives: 54 us -> 52 us
    unnamed x30 -> x24, local copies, waits for them, and re-layouts: 8.42 us -> 4.51 us
    all_to_all x2, waiting for transfers between devices: 17.5 us -> 20.5 us  [exchange(): lax.all_to_all(pieces, ('blk', 'sp'), split_axis=0, concat_axis=0, tiled=...]
    all_to_all x2, blocking collectives: 54 us -> 52 us  [exchange(): lax.all_to_all(pieces, ('blk', 'sp'), split_axis=0, concat_axis=0, tiled=...]
  transfers between devices with their start and end apart: 2 -> 2, of which waited for: 2 -> 2; matrix products, arithmetic and copies ran while one was open for 0% -> 0% of each run, Pallas kernels for 13% -> 14%
where the time goes in v3:
time: 127 us; the launch traced here: 126 us
  blocking collectives  52 us (41%)
  Pallas kernels  27.6 us (22%)
  starting transfers between devices  21 us (17%)
  waiting for transfers between devices  20.5 us (16%)
  local copies, waits for them, and re-layouts  4.51 us (4%)
    all_to_all x2, blocking collectives, exchange(): lax.all_to_all(pieces, ('blk', 'sp'), split_axis=0, concat_axis=0, tiled=...  52 us
    all_to_all x2, starting transfers between devices, exchange(): lax.all_to_all(pieces, ('blk', 'sp'), split_axis=0, concat_axis=0, tiled=...  21 us
    all_to_all x2, waiting for transfers between devices, exchange(): lax.all_to_all(pieces, ('blk', 'sp'), split_axis=0, concat_axis=0, tiled=...  20.5 us
    pallas_call x1, Pallas kernels, rest_part(): pl.pallas_call(rest_kernel, grid=(KEY_VALUE_HEADS,), out_shape=(rows, row...  11.3 us
    pallas_call x1, Pallas kernels, own_part(): pl.pallas_call(own_kernel, grid=(KEY_VALUE_HEADS,), out_shape=(pltpu.HBM(...  6.07 us
    pallas_call x1, Pallas kernels, listed_part(): pl.pallas_call(listed_kernel, out_shape=(shape(SLICES, BLOCK, HEAD_SIZE),...  4.58 us
    unnamed x24, local copies, waits for them, and re-layouts  4.51 us
  transfers between devices with their start and end apart: 2, of which 2 were waited for; matrix products, arithmetic and copies ran while one was open for 0% of the time, Pallas kernels for 14%

profile of v3, /device:TPU:1, one launch (start us, length us, event | category | flops | bytes accessed | tf_op | source)
XLA Modules:
  0.0 126.4 jit_solution(12695527524765903904)
XLA Ops:
  0.6 0.0 copy-start.9
  0.6 0.0 copy-start
  0.7 0.0 copy-start.11
  0.7 2.5 %pack.1.pair_ref.own_ref = bf16[16,128,128]{2,1,0:T(8,128)(2,1)} custom-call(s32[8,16]{1,0:T(8,128)} %bitcast.16, s32[8,16]{1,0:T(8,128)} %bitcast.17, bf16[128,128]{1,0:T(8,128)(2,1)} %constant.2.clone.hadamard_ref, bf16[128,1024]{1,0:T(8,128)(2,1)} %key_ref.1, bf16[128,1024]{1,0:T(8,128)(2,1)} %value_ref.1), custom_call_target="tpu_custom_call" | custom-call | tf_op jit(solution)/shard_map/pack/pallas_call | solution.py:293
  3.2 15.7 %all-to-all-start = ((bf16[256,8,128]{2,1,0:T(8,128)(2,1)}), bf16[256,8,128]{2,1,0:T(8,128)(2,1)S(1)}, u32[]{:S(2)}, u32[]{:S(2)}) async-start(bf16[256,8,128]{2,1,0:T(8,128)(2,1)} %bitcast.7), calls=%async_computation | async-start | bytes 1048576 | tf_op jit(solution)/shard_map/all_to_all | solution.py:373
  18.8 0.0 copy-done.9
  18.8 0.0 copy-done
  18.8 0.0 copy-done.11
  18.8 0.0 copy-start.1
  18.9 1.1 copy-done.1
  19.9 0.0 copy-start.3
  19.9 1.6 %copy-done.3 = bf16[128,8192]{1,0:T(8,128)(2,1)S(1)} copy-done((bf16[128,8192]{1,0:T(8,128)(2,1)S(1)}, bf16[128,8192]{1,0:T(8,128)(2,1)}, u32[]{:S(2)}) %copy-start.3) | copy-done | bytes 2097176
  21.5 0.0 copy-start.10
  21.5 6.1 %own_part.1 = (bf16[8,1024,128]{2,1,0:T(8,128)(2,1)}, f32[8,8,1024]{2,1,0:T(8,128)S(1)}) custom-call(s32[16,64]{1,0:T(8,128)S(1)} %copy-done.11, bf16[128,128]{1,0:T(8,128)(2,1)S(1)} %copy-done.9, bf16[128,8192]{1,0:T(8,128)(2,1)S(1)} %copy-done.3, bf16[128,8192]{1,0:T(8,128)(2,1)S(1)} %copy-done, bf16[16,128,128]{2,1,0:T(8,128)(2,1)S(1)} %copy-done.1), custom_call_target="tpu_custom_call" | custom-call | flops 805306368 | bytes 7340032 | tf_op jit(solution)/shard_map/own_part/pallas_call | solution.py:331
  27.6 12.1 %all-to-all-done.source_ref = bf16[256,8,128]{2,1,0:T(8,128)(2,1)S(1)} async-done(((bf16[256,8,128]{2,1,0:T(8,128)(2,1)}), bf16[256,8,128]{2,1,0:T(8,128)(2,1)S(1)}, u32[]{:S(2)}, u32[]{:S(2)}) %all-to-all-start) | async-done | bytes 524320 | tf_op jit(solution)/shard_map/all_to_all | solution.py:373
  39.6 0.0 copy-start.4
  39.6 0.0 copy-done.10
  39.7 0.9 pick.1
  40.6 26.0 %all_to_all.20 = bf16[256,8,128]{2,1,0:T(8,128)(2,1)S(1)} all-to-all(bf16[256,8,128]{2,1,0:T(8,128)(2,1)S(1)} %pick.1), channel_id=1, replica_groups=mesh['sp'=16,'blk'=16] {'blk','sp'}, dimensions={0} | all-to-all | bytes 1048576 | tf_op jit(solution)/shard_map/all_to_all | solution.py:373
  66.5 0.0 copy-start.5
  66.6 0.0 copy-done.4
  66.6 0.0 copy-start.2
  66.6 4.6 %listed_part.1 = (bf16[16,128,128]{2,1,0:T(8,128)(2,1)S(1)}, f32[8,8,1024]{2,1,0:T(8,128)S(1)}) custom-call(s32[256]{0:T(256)S(1)} %bitcast.13, bf16[128,128]{1,0:T(8,128)(2,1)S(1)} %copy-done.9, bf16[8,1024,128]{2,1,0:T(8,128)(2,1)S(1)} %copy-done.4, bf16[128,8192]{1,0:T(8,128)(2,1)S(1)} %copy-done, bf16[16,128,128]{2,1,0:T(8,128)(2,1)S(1)} %bitcast.9, ...), custom_call_target="tpu_custom_call" | custom-call | flops 1073741824 | bytes 6291456 | tf_op jit(solution)/shard_map/listed_part/pallas_call | solution.py:344
  71.1 0.0 copy-done.5
  71.2 0.0 copy-start.8
  71.2 0.8 copy-done.8
  71.9 5.4 %all-to-all-start.2 = ((bf16[256,8,128]{2,1,0:T(8,128)(2,1)}), bf16[256,8,128]{2,1,0:T(8,128)(2,1)S(1)}, u32[]{:S(2)}, u32[]{:S(2)}) async-start(bf16[256,8,128]{2,1,0:T(8,128)(2,1)} %bitcast.11), calls=%async_computation.2 | async-start | bytes 1048576 | tf_op jit(solution)/shard_map/all_to_all | solution.py:373
  77.3 0.0 copy-done.2
  77.3 0.0 copy-start.6
  77.3 1.0 copy-done.6
  78.4 11.3 %rest_part.1 = (bf16[128,8192]{1,0:T(8,128)(2,1)}, bf16[128,8192]{1,0:T(8,128)(2,1)}, f32[16,128,128]{2,1,0:T(8,128)}) custom-call(s32[256]{0:T(256)S(1)} %bitcast.14, bf16[128,128]{1,0:T(8,128)(2,1)S(1)} %copy-done.9, bf16[8,1024,128]{2,1,0:T(8,128)(2,1)} %get-tuple-element.22.deq_ref, bf16[128,8192]{1,0:T(8,128)(2,1)S(1)} %copy-done, ...), custom_call_target="tpu_custom_call" | custom-call | flops 2684354560 | bytes 11534336 | tf_op jit(solution)/shard_map/rest_part/pallas_call | solution.py:359
  89.7 0.0 copy-start.7
  89.7 8.5 %all-to-all-done.2.part_ref = bf16[256,8,128]{2,1,0:T(8,128)(2,1)S(1)} async-done(((bf16[256,8,128]{2,1,0:T(8,128)(2,1)}), bf16[256,8,128]{2,1,0:T(8,128)(2,1)S(1)}, u32[]{:S(2)}, u32[]{:S(2)}) %all-to-all-start.2) | async-done | bytes 524320 | tf_op jit(solution)/shard_map/all_to_all | solution.py:373
  98.1 1.3 %accumulate.1 = bf16[256,8,128]{2,1,0:T(8,128)(2,1)S(1)} custom-call(s32[256]{0:T(256)S(1)} %bitcast.15, bf16[256,8,128]{2,1,0:T(8,128)(2,1)S(1)} %all-to-all-done.2.part_ref), custom_call_target="tpu_custom_call" | custom-call | tf_op jit(solution)/shard_map/accumulate/pallas_call | solution.py:281
  99.5 26.0 %all_to_all.21 = bf16[256,8,128]{2,1,0:T(8,128)(2,1)S(1)} all-to-all(bf16[256,8,128]{2,1,0:T(8,128)(2,1)S(1)} %accumulate.1), channel_id=1, replica_groups=mesh['sp'=16,'blk'=16] {'blk','sp'}, dimensions={0} | all-to-all | bytes 1048576 | tf_op jit(solution)/shard_map/all_to_all | solution.py:373
  125.5 0.0 copy-done.7
  125.5 0.9 finish.1
Async XLA Ops:
  0.6 18.2 %copy-start.9 = (bf16[128,128]{1,0:T(8,128)(2,1)S(1)}, bf16[128,128]{1,0:T(8,128)(2,1)}, u32[]{:S(2)}) copy-start(bf16[128,128]{1,0:T(8,128)(2,1)} %constant.2.clone.hadamard_ref) | copy-start | bytes 98308
  0.6 18.2 %copy-start = (bf16[128,8192]{1,0:T(8,128)(2,1)S(1)}, bf16[128,8192]{1,0:T(8,128)(2,1)}, u32[]{:S(2)}) copy-start(bf16[128,8192]{1,0:T(8,128)(2,1)} %grad_ref.5) | copy-start | bytes 6291460
  0.7 18.2 %copy-start.11 = (s32[16,64]{1,0:T(8,128)S(1)}, s32[16,64]{1,0:T(8,128)}, u32[]{:S(2)}) copy-start(s32[16,64]{1,0:T(8,128)} %exponent.1) | copy-start | bytes 12292
  3.2 36.5 %all-to-all-start = ((bf16[256,8,128]{2,1,0:T(8,128)(2,1)}), bf16[256,8,128]{2,1,0:T(8,128)(2,1)S(1)}, u32[]{:S(2)}, u32[]{:S(2)}) async-start(bf16[256,8,128]{2,1,0:T(8,128)(2,1)} %bitcast.7), calls=%async_computation | async-start | bytes 1048576 | tf_op jit(solution)/shard_map/all_to_all | solution.py:373
  18.8 1.1 copy-start.1
  19.9 1.6 %copy-start.3 = (bf16[128,8192]{1,0:T(8,128)(2,1)S(1)}, bf16[128,8192]{1,0:T(8,128)(2,1)}, u32[]{:S(2)}) copy-start(bf16[128,8192]{1,0:T(8,128)(2,1)} %query_ref.1) | copy-start | bytes 6291460
  21.5 18.1 %copy-start.10 = (s32[256,1]{0,1:T(1,128)S(1)}, s32[256,1]{0,1:T(1,128)}, u32[]{:S(2)}) copy-start(s32[256,1]{0,1:T(1,128)} %param.13) | copy-start | bytes 3076
  39.6 26.9 %copy-start.4 = (bf16[8,1024,128]{2,1,0:T(8,128)(2,1)S(1)}, bf16[8,1024,128]{2,1,0:T(8,128)(2,1)}, u32[]{:S(2)}) copy-start(bf16[8,1024,128]{2,1,0:T(8,128)(2,1)} %get-tuple-element.22.deq_ref) | copy-start | bytes 6291460
  66.5 4.6 %copy-start.5 = (bf16[256,8,128]{2,1,0:T(8,128)(2,1)}, bf16[256,8,128]{2,1,0:T(8,128)(2,1)S(1)}, u32[]{:S(2)}) copy-start(bf16[256,8,128]{2,1,0:T(8,128)(2,1)S(1)} %all_to_all.20) | copy-start | bytes 1572868
  66.6 10.8 %copy-start.2 = (bf16[16,128,128]{2,1,0:T(8,128)(2,1)S(1)}, bf16[16,128,128]{2,1,0:T(8,128)(2,1)}, u32[]{:S(2)}) copy-start(bf16[16,128,128]{2,1,0:T(8,128)(2,1)} %pack.1.pair_ref.own_ref) | copy-start | bytes 1572868
  71.2 0.8 copy-start.8
  71.9 26.2 %all-to-all-start.2 = ((bf16[256,8,128]{2,1,0:T(8,128)(2,1)}), bf16[256,8,128]{2,1,0:T(8,128)(2,1)S(1)}, u32[]{:S(2)}, u32[]{:S(2)}) async-start(bf16[256,8,128]{2,1,0:T(8,128)(2,1)} %bitcast.11), calls=%async_computation.2 | async-start | bytes 1048576 | tf_op jit(solution)/shard_map/all_to_all | solution.py:373
  77.3 1.0 copy-start.6
  89.7 35.8 %copy-start.7 = (f32[16,128,128]{2,1,0:T(8,128)S(1)}, f32[16,128,128]{2,1,0:T(8,128)}, u32[]{:S(2)}) copy-start(f32[16,128,128]{2,1,0:T(8,128)} %get-tuple-element.32.own_ref) | copy-start | bytes 3145732

commit v4 on v3

--- a/solution.py
+++ b/solution.py
@@ -18,6 +18,7 @@
 PIECE = 8
 MAX_CODE = 448.0
 SCORE_SCALE = 1.0 / (HEAD_SIZE * math.sqrt(HEAD_SIZE))
+LOG_SCALE = SCORE_SCALE * math.log2(math.e)
 BF16 = jnp.bfloat16
 F32 = jnp.float32
 CHUNK = 256
@@ -93,13 +94,8 @@
 
 
 def pick_kernel(index, source_ref, out_ref):
-    def some(step, carry):
-        for place in range(UNROLL):
-            row = step * UNROLL + place
-            out_ref[row] = source_ref[index[row]]
-        return carry
-
-    lax.fori_loop(0, out_ref.shape[0] // UNROLL, some, 0)
+    for row in range(out_ref.shape[0]):
+        out_ref[row] = source_ref[index[row]]
 
 
 def accumulate_kernel(index, part_ref, out_ref, even, odd):
@@ -118,7 +114,7 @@
 
 
 def finish_kernel(own_ref, listed_ref, key_ref, value_ref):
-    for head in range(KEY_VALUE_HEADS):
+    for head in range(KEY_VALUE_HEADS // 2):
         cols = slice(head * HEAD_SIZE, (head + 1) * HEAD_SIZE)
         total = own_ref[2 * head : 2 * head + 2] + listed_ref[2 * head : 2 * head + 2].astype(F32)
         key_ref[:, cols] = total[0].astype(BF16)
@@ -140,10 +136,10 @@
         deq_ref[0, head * BLOCK : (head + 1) * BLOCK, :] = quantize(
             lanes(query_ref, head), hadamard, power(-level, 1, 0.5), power(level, 5, 1.0 / 32.0)
         )
-    scores = matmul_nt(pair_ref[0], deq_ref[0]) * SCORE_SCALE
+    scores = matmul_nt(pair_ref[0], deq_ref[0]) * LOG_SCALE
     scores = jnp.where(causal_mask(), scores, -jnp.inf)
     top = jnp.max(scores, axis=0, keepdims=True)
-    weights = jnp.exp(scores - top)
+    weights = jnp.exp2(scores - top)
     prob_grad = matmul_nt(pair_ref[1], stack_heads(grad_ref))
     stats_ref[0, 0:1, :] = top
     stats_ref[0, 1:2, :] = jnp.sum(weights, axis=0, keepdims=True)
@@ -170,18 +166,18 @@
         scores = matmul_nt(pair_ref[2 * head], deq_ref[head, cols, :])
         prob_grad = matmul_nt(pair_ref[2 * head + 1], grad)
         own_top = stats_ref[head, 0:1, cols]
-        best = jnp.max(scores, axis=0, keepdims=True) * SCORE_SCALE
+        best = jnp.max(scores, axis=0, keepdims=True) * LOG_SCALE
         top = jnp.maximum(own_top, jnp.where(listed, best, -jnp.inf))
-        weights = jnp.exp(scores * SCORE_SCALE - jnp.where(listed, top, jnp.inf))
-        shrink = jnp.exp(own_top - top)
+        weights = jnp.exp2(scores * LOG_SCALE - jnp.where(listed, top, jnp.inf))
+        shrink = jnp.exp2(own_top - top)
         inverse = 1.0 / (
             stats_ref[head, 1:2, cols] * shrink + jnp.sum(weights, axis=0, keepdims=True)
         )
         delta = stats_ref[head, 2:3, cols] * shrink
         delta = (delta + jnp.sum(weights * prob_grad, axis=0, keepdims=True)) * inverse
-        scaled = inverse * SCORE_SCALE
-        prob_scr[slot, :, cols] = (weights * inverse).astype(BF16)
-        score_scr[slot, :, cols] = (weights * (prob_grad * scaled - delta * scaled)).astype(BF16)
+        probs = weights * inverse
+        prob_scr[slot, :, cols] = probs.astype(BF16)
+        score_scr[slot, :, cols] = (probs * (prob_grad - delta)).astype(BF16)
         final_ref[head, 0:1, cols] = top
         final_ref[head, 1:2, cols] = inverse
         final_ref[head, 2:3, cols] = delta
@@ -197,8 +193,8 @@
                 softmax(head, head % 2, start)
         if head > 0:
             last, slot = head - 1, (head - 1) % 2
-            key_sum = matmul(score_scr[slot], deq_ref[last]).astype(BF16)
-            pair_out[2 * last] = matmul(key_sum, hadamard_ref[...]).astype(BF16)
+            key_sum = matmul(score_scr[slot], deq_ref[last]) * SCORE_SCALE
+            pair_out[2 * last] = matmul(key_sum.astype(BF16), hadamard_ref[...]).astype(BF16)
             value_sum = matmul(prob_scr[slot], grad_rows(last, 0, GROUP))
             pair_out[2 * last + 1] = value_sum.astype(BF16)
 
@@ -229,8 +225,8 @@
     delta = final_ref[0, 2:3, :]
 
     def part(key, value, mask):
-        scores = matmul_nt(key, deq) * SCORE_SCALE
-        probs = jnp.exp(jnp.where(mask, scores, -jnp.inf) - top) * inverse
+        scores = matmul_nt(key, deq) * LOG_SCALE
+        probs = jnp.exp2(jnp.where(mask, scores, -jnp.inf) - top) * inverse
         prob_grad = matmul_nt(value, grad)
         score_grad = (probs * (prob_grad - delta) * SCORE_SCALE).astype(BF16)
         return probs.astype(BF16), score_grad
@@ -302,11 +298,14 @@
 
 def finish(own, listed):
     out = shape(BLOCK, KEY_VALUE_HEADS * HEAD_SIZE)
+    pairs = pl.BlockSpec((SLICES // 2, BLOCK, HEAD_SIZE), lambda half: (half, 0, 0))
+    rows = pl.BlockSpec((BLOCK, KEY_VALUE_HEADS * HEAD_SIZE // 2), lambda half: (0, half))
     return pl.pallas_call(
         finish_kernel,
+        grid=(2,),
         out_shape=(out, out),
-        in_specs=[vmem(), vmem()],
-        out_specs=(vmem(), vmem()),
+        in_specs=[pairs, pairs],
+        out_specs=(rows, rows),
         compiler_params=params(),
         name="finish",
     )(own, listed)

time: 127 us -> 126 us (level)
  Pallas kernels: 27.6 us -> 26.3 us
  transfers between devices with their start and end apart: 2 -> 2, of which waited for: 2 -> 2; matrix products, arithmetic and copies ran while one was open for 0% -> 0% of each run, Pallas kernels for 14% -> 13%
where the time goes in v4:
time: 126 us
  blocking collectives  52 us (41%)
  Pallas kernels  26.3 us (21%)
  waiting for transfers between devices  21.2 us (17%)
  starting transfers between devices  21 us (17%)
  local copies, waits for them, and re-layouts  4.51 us (4%)
    all_to_all x2, blocking collectives, exchange(): lax.all_to_all(pieces, ('blk', 'sp'), split_axis=0, concat_axis=0, tiled=...  52 us
    all_to_all x2, waiting for transfers between devices, exchange(): lax.all_to_all(pieces, ('blk', 'sp'), split_axis=0, concat_axis=0, tiled=...  21.2 us
    all_to_all x2, starting transfers between devices, exchange(): lax.all_to_all(pieces, ('blk', 'sp'), split_axis=0, concat_axis=0, tiled=...  21 us
    pallas_call x1, Pallas kernels, rest_part(): pl.pallas_call(rest_kernel, grid=(KEY_VALUE_HEADS,), out_shape=(rows, row...  10.8 us
    pallas_call x1, Pallas kernels, own_part(): pl.pallas_call(own_kernel, grid=(KEY_VALUE_HEADS,), out_shape=(pltpu.HBM(...  5.94 us
    unnamed x24, local copies, waits for them, and re-layouts  4.51 us
    pallas_call x1, Pallas kernels, listed_part(): pl.pallas_call(listed_kernel, out_shape=(shape(SLICES, BLOCK, HEAD_SIZE),...  4.2 us
  transfers between devices with their start and end apart: 2, of which 2 were waited for; matrix products, arithmetic and copies ran while one was open for 0% of the time, Pallas kernels for 13%

profile of v4, /device:TPU:1, one launch (start us, length us, event | category | flops | bytes accessed | tf_op | source)
XLA Modules:
  0.0 125.8 jit_solution(723274514148223306)
XLA Ops:
  0.6 0.0 copy-start.9
  0.6 0.0 copy-start
  0.7 0.0 copy-start.11
  0.7 2.5 %pack.1.pair_ref.own_ref = bf16[16,128,128]{2,1,0:T(8,128)(2,1)} custom-call(s32[8,16]{1,0:T(8,128)} %bitcast.16, s32[8,16]{1,0:T(8,128)} %bitcast.17, bf16[128,128]{1,0:T(8,128)(2,1)} %constant.2.clone.hadamard_ref, bf16[128,1024]{1,0:T(8,128)(2,1)} %key_ref.1, bf16[128,1024]{1,0:T(8,128)(2,1)} %value_ref.1), custom_call_target="tpu_custom_call" | custom-call | tf_op jit(solution)/shard_map/pack/pallas_call | solution.py:289
  3.2 15.7 %all-to-all-start = ((bf16[256,8,128]{2,1,0:T(8,128)(2,1)}), bf16[256,8,128]{2,1,0:T(8,128)(2,1)S(1)}, u32[]{:S(2)}, u32[]{:S(2)}) async-start(bf16[256,8,128]{2,1,0:T(8,128)(2,1)} %bitcast.7), calls=%async_computation | async-start | bytes 1048576 | tf_op jit(solution)/shard_map/all_to_all | solution.py:372
  18.8 0.0 copy-done.9
  18.8 0.0 copy-done
  18.8 0.0 copy-done.11
  18.8 0.0 copy-start.1
  18.9 1.1 copy-done.1
  19.9 0.0 copy-start.3
  19.9 1.6 %copy-done.3 = bf16[128,8192]{1,0:T(8,128)(2,1)S(1)} copy-done((bf16[128,8192]{1,0:T(8,128)(2,1)S(1)}, bf16[128,8192]{1,0:T(8,128)(2,1)}, u32[]{:S(2)}) %copy-start.3) | copy-done | bytes 2097176
  21.5 0.0 copy-start.10
  21.5 5.9 %own_part.1 = (bf16[8,1024,128]{2,1,0:T(8,128)(2,1)}, f32[8,8,1024]{2,1,0:T(8,128)S(1)}) custom-call(s32[16,64]{1,0:T(8,128)S(1)} %copy-done.11, bf16[128,128]{1,0:T(8,128)(2,1)S(1)} %copy-done.9, bf16[128,8192]{1,0:T(8,128)(2,1)S(1)} %copy-done.3, bf16[128,8192]{1,0:T(8,128)(2,1)S(1)} %copy-done, bf16[16,128,128]{2,1,0:T(8,128)(2,1)S(1)} %copy-done.1), custom_call_target="tpu_custom_call" | custom-call | flops 805306368 | bytes 7340032 | tf_op jit(solution)/shard_map/own_part/pallas_call | solution.py:330
  27.5 12.2 %all-to-all-done.source_ref = bf16[256,8,128]{2,1,0:T(8,128)(2,1)S(1)} async-done(((bf16[256,8,128]{2,1,0:T(8,128)(2,1)}), bf16[256,8,128]{2,1,0:T(8,128)(2,1)S(1)}, u32[]{:S(2)}, u32[]{:S(2)}) %all-to-all-start) | async-done | bytes 524320 | tf_op jit(solution)/shard_map/all_to_all | solution.py:372
  39.6 0.0 copy-start.4
  39.6 0.0 copy-done.10
  39.7 0.8 pick.1
  40.4 26.0 %all_to_all.20 = bf16[256,8,128]{2,1,0:T(8,128)(2,1)S(1)} all-to-all(bf16[256,8,128]{2,1,0:T(8,128)(2,1)S(1)} %pick.1), channel_id=1, replica_groups=mesh['sp'=16,'blk'=16] {'blk','sp'}, dimensions={0} | all-to-all | bytes 1048576 | tf_op jit(solution)/shard_map/all_to_all | solution.py:372
  66.4 0.0 copy-start.5
  66.4 0.0 copy-done.4
  66.4 0.0 copy-start.2
  66.4 4.2 %listed_part.1 = (bf16[16,128,128]{2,1,0:T(8,128)(2,1)S(1)}, f32[8,8,1024]{2,1,0:T(8,128)S(1)}) custom-call(s32[256]{0:T(256)S(1)} %bitcast.13, bf16[128,128]{1,0:T(8,128)(2,1)S(1)} %copy-done.9, bf16[8,1024,128]{2,1,0:T(8,128)(2,1)S(1)} %copy-done.4, bf16[128,8192]{1,0:T(8,128)(2,1)S(1)} %copy-done, bf16[16,128,128]{2,1,0:T(8,128)(2,1)S(1)} %bitcast.9, ...), custom_call_target="tpu_custom_call" | custom-call | flops 1073741824 | bytes 6291456 | tf_op jit(solution)/shard_map/listed_part/pallas_call | solution.py:343
  70.6 0.0 copy-done.5
  70.6 0.0 copy-start.8
  70.6 0.8 copy-done.8
  71.4 5.4 %all-to-all-start.2 = ((bf16[256,8,128]{2,1,0:T(8,128)(2,1)}), bf16[256,8,128]{2,1,0:T(8,128)(2,1)S(1)}, u32[]{:S(2)}, u32[]{:S(2)}) async-start(bf16[256,8,128]{2,1,0:T(8,128)(2,1)} %bitcast.11), calls=%async_computation.2 | async-start | bytes 1048576 | tf_op jit(solution)/shard_map/all_to_all | solution.py:372
  76.8 0.0 copy-done.2
  76.8 0.0 copy-start.6
  76.8 1.0 copy-done.6
  77.9 10.8 %rest_part.1 = (bf16[128,8192]{1,0:T(8,128)(2,1)}, bf16[128,8192]{1,0:T(8,128)(2,1)}, f32[16,128,128]{2,1,0:T(8,128)}) custom-call(s32[256]{0:T(256)S(1)} %bitcast.14, bf16[128,128]{1,0:T(8,128)(2,1)S(1)} %copy-done.9, bf16[8,1024,128]{2,1,0:T(8,128)(2,1)} %get-tuple-element.22.deq_ref, bf16[128,8192]{1,0:T(8,128)(2,1)S(1)} %copy-done, ...), custom_call_target="tpu_custom_call" | custom-call | flops 2684354560 | bytes 11534336 | tf_op jit(solution)/shard_map/rest_part/pallas_call | solution.py:358
  88.6 0.0 copy-start.7
  88.6 9.0 %all-to-all-done.2.part_ref = bf16[256,8,128]{2,1,0:T(8,128)(2,1)S(1)} async-done(((bf16[256,8,128]{2,1,0:T(8,128)(2,1)}), bf16[256,8,128]{2,1,0:T(8,128)(2,1)S(1)}, u32[]{:S(2)}, u32[]{:S(2)}) %all-to-all-start.2) | async-done | bytes 524320 | tf_op jit(solution)/shard_map/all_to_all | solution.py:372
  97.6 1.3 %accumulate.1 = bf16[256,8,128]{2,1,0:T(8,128)(2,1)S(1)} custom-call(s32[256]{0:T(256)S(1)} %bitcast.15, bf16[256,8,128]{2,1,0:T(8,128)(2,1)S(1)} %all-to-all-done.2.part_ref), custom_call_target="tpu_custom_call" | custom-call | tf_op jit(solution)/shard_map/accumulate/pallas_call | solution.py:277
  99.0 26.0 %all_to_all.21 = bf16[256,8,128]{2,1,0:T(8,128)(2,1)S(1)} all-to-all(bf16[256,8,128]{2,1,0:T(8,128)(2,1)S(1)} %accumulate.1), channel_id=1, replica_groups=mesh['sp'=16,'blk'=16] {'blk','sp'}, dimensions={0} | all-to-all | bytes 1048576 | tf_op jit(solution)/shard_map/all_to_all | solution.py:372
  125.0 0.0 copy-done.7
  125.0 0.8 finish.1
Async XLA Ops:
  0.6 18.2 %copy-start.9 = (bf16[128,128]{1,0:T(8,128)(2,1)S(1)}, bf16[128,128]{1,0:T(8,128)(2,1)}, u32[]{:S(2)}) copy-start(bf16[128,128]{1,0:T(8,128)(2,1)} %constant.2.clone.hadamard_ref) | copy-start | bytes 98308
  0.6 18.2 %copy-start = (bf16[128,8192]{1,0:T(8,128)(2,1)S(1)}, bf16[128,8192]{1,0:T(8,128)(2,1)}, u32[]{:S(2)}) copy-start(bf16[128,8192]{1,0:T(8,128)(2,1)} %grad_ref.5) | copy-start | bytes 6291460
  0.7 18.2 %copy-start.11 = (s32[16,64]{1,0:T(8,128)S(1)}, s32[16,64]{1,0:T(8,128)}, u32[]{:S(2)}) copy-start(s32[16,64]{1,0:T(8,128)} %exponent.1) | copy-start | bytes 12292
  3.2 36.5 %all-to-all-start = ((bf16[256,8,128]{2,1,0:T(8,128)(2,1)}), bf16[256,8,128]{2,1,0:T(8,128)(2,1)S(1)}, u32[]{:S(2)}, u32[]{:S(2)}) async-start(bf16[256,8,128]{2,1,0:T(8,128)(2,1)} %bitcast.7), calls=%async_computation | async-start | bytes 1048576 | tf_op jit(solution)/shard_map/all_to_all | solution.py:372
  18.8 1.1 copy-start.1
  19.9 1.6 %copy-start.3 = (bf16[128,8192]{1,0:T(8,128)(2,1)S(1)}, bf16[128,8192]{1,0:T(8,128)(2,1)}, u32[]{:S(2)}) copy-start(bf16[128,8192]{1,0:T(8,128)(2,1)} %query_ref.1) | copy-start | bytes 6291460
  21.5 18.1 %copy-start.10 = (s32[256,1]{0,1:T(1,128)S(1)}, s32[256,1]{0,1:T(1,128)}, u32[]{:S(2)}) copy-start(s32[256,1]{0,1:T(1,128)} %param.13) | copy-start | bytes 3076
  39.6 26.8 %copy-start.4 = (bf16[8,1024,128]{2,1,0:T(8,128)(2,1)S(1)}, bf16[8,1024,128]{2,1,0:T(8,128)(2,1)}, u32[]{:S(2)}) copy-start(bf16[8,1024,128]{2,1,0:T(8,128)(2,1)} %get-tuple-element.22.deq_ref) | copy-start | bytes 6291460
  66.4 4.2 %copy-start.5 = (bf16[256,8,128]{2,1,0:T(8,128)(2,1)}, bf16[256,8,128]{2,1,0:T(8,128)(2,1)S(1)}, u32[]{:S(2)}) copy-start(bf16[256,8,128]{2,1,0:T(8,128)(2,1)S(1)} %all_to_all.20) | copy-start | bytes 1572868
  66.4 10.4 %copy-start.2 = (bf16[16,128,128]{2,1,0:T(8,128)(2,1)S(1)}, bf16[16,128,128]{2,1,0:T(8,128)(2,1)}, u32[]{:S(2)}) copy-start(bf16[16,128,128]{2,1,0:T(8,128)(2,1)} %pack.1.pair_ref.own_ref) | copy-start | bytes 1572868
  70.6 0.8 copy-start.8
  71.4 26.2 %all-to-all-start.2 = ((bf16[256,8,128]{2,1,0:T(8,128)(2,1)}), bf16[256,8,128]{2,1,0:T(8,128)(2,1)S(1)}, u32[]{:S(2)}, u32[]{:S(2)}) async-start(bf16[256,8,128]{2,1,0:T(8,128)(2,1)} %bitcast.11), calls=%async_computation.2 | async-start | bytes 1048576 | tf_op jit(solution)/shard_map/all_to_all | solution.py:372
  76.8 1.0 copy-start.6
  88.6 36.3 %copy-start.7 = (f32[16,128,128]{2,1,0:T(8,128)S(1)}, f32[16,128,128]{2,1,0:T(8,128)}, u32[]{:S(2)}) copy-start(f32[16,128,128]{2,1,0:T(8,128)} %get-tuple-element.32.own_ref) | copy-start | bytes 3145732

commit v5 on v4

--- a/solution.py
+++ b/solution.py
@@ -73,21 +73,22 @@
     hadamard = hadamard_ref[...]
     row = lax.axis_index("sp")
 
-    def coded(ref, exponent_ref):
-        stacked = jnp.concatenate([lanes(ref, head) for head in range(KEY_VALUE_HEADS)], axis=0)
-        rotated = matmul(stacked, hadamard)
+    stacked = [lanes(ref, head) for ref in (value_ref, key_ref) for head in range(KEY_VALUE_HEADS)]
+    rotated = matmul(jnp.concatenate(stacked, axis=0), hadamard)
+
+    def coded(first, exponent_ref):
         down, up = own_powers(exponent_ref[...], row)
         parts = []
         for head in range(KEY_VALUE_HEADS):
             one = slice(head, head + 1)
-            part = rotated[head * BLOCK : (head + 1) * BLOCK] * down[one, :]
+            part = rotated[(first + head) * BLOCK : (first + head + 1) * BLOCK] * down[one, :]
             part = jnp.clip(part, -MAX_CODE, MAX_CODE).astype(BF16)
             parts.append((part.astype(F32) * up[one, :]).astype(BF16))
         return parts
 
-    keys = coded(key_ref, key_exponent)
-    values = matmul(jnp.concatenate(coded(value_ref, value_exponent), axis=0), hadamard)
+    values = matmul(jnp.concatenate(coded(0, value_exponent), axis=0), hadamard)
     values = (values * (1.0 / HEAD_SIZE)).astype(BF16)
+    keys = coded(KEY_VALUE_HEADS, key_exponent)
     for head in range(KEY_VALUE_HEADS):
         out_ref[2 * head] = keys[head]
         out_ref[2 * head + 1] = values[head * BLOCK : (head + 1) * BLOCK]

time: 126 us -> 126 us (level)
  no operation moved by 1% of the time
where the time goes in v5:
time: 126 us
  blocking collectives  52 us (41%)
  Pallas kernels  26.3 us (21%)
  waiting for transfers between devices  21.2 us (17%)
  starting transfers between devices  21 us (17%)
  local copies, waits for them, and re-layouts  4.51 us (4%)
    all_to_all x2, blocking collectives, exchange(): lax.all_to_all(pieces, ('blk', 'sp'), split_axis=0, concat_axis=0, tiled=...  52 us
    all_to_all x2, waiting for transfers between devices, exchange(): lax.all_to_all(pieces, ('blk', 'sp'), split_axis=0, concat_axis=0, tiled=...  21.2 us
    all_to_all x2, starting transfers between devices, exchange(): lax.all_to_all(pieces, ('blk', 'sp'), split_axis=0, concat_axis=0, tiled=...  21 us
    pallas_call x1, Pallas kernels, rest_part(): pl.pallas_call(rest_kernel, grid=(KEY_VALUE_HEADS,), out_shape=(rows, row...  10.8 us
    pallas_call x1, Pallas kernels, own_part(): pl.pallas_call(own_kernel, grid=(KEY_VALUE_HEADS,), out_shape=(pltpu.HBM(...  5.94 us
    unnamed x24, local copies, waits for them, and re-layouts  4.51 us
    pallas_call x1, Pallas kernels, listed_part(): pl.pallas_call(listed_kernel, out_shape=(shape(SLICES, BLOCK, HEAD_SIZE),...  4.2 us
  transfers between devices with their start and end apart: 2, of which 2 were waited for; matrix products, arithmetic and copies ran while one was open for 0% of the time, Pallas kernels for 13%

profile of v5, /device:TPU:1, one launch (start us, length us, event | category | flops | bytes accessed | tf_op | source)
XLA Modules:
  0.0 125.7 jit_solution(8516436270283674539)
XLA Ops:
  0.6 0.0 copy-start.9
  0.6 0.0 copy-start
  0.7 0.0 copy-start.11
  0.7 2.4 %pack.1.pair_ref.own_ref = bf16[16,128,128]{2,1,0:T(8,128)(2,1)} custom-call(s32[8,16]{1,0:T(8,128)} %bitcast.16, s32[8,16]{1,0:T(8,128)} %bitcast.17, bf16[128,128]{1,0:T(8,128)(2,1)} %constant.2.clone.hadamard_ref, bf16[128,1024]{1,0:T(8,128)(2,1)} %key_ref.1, bf16[128,1024]{1,0:T(8,128)(2,1)} %value_ref.1), custom_call_target="tpu_custom_call" | custom-call | tf_op jit(solution)/shard_map/pack/pallas_call | solution.py:290
  3.1 15.7 %all-to-all-start = ((bf16[256,8,128]{2,1,0:T(8,128)(2,1)}), bf16[256,8,128]{2,1,0:T(8,128)(2,1)S(1)}, u32[]{:S(2)}, u32[]{:S(2)}) async-start(bf16[256,8,128]{2,1,0:T(8,128)(2,1)} %bitcast.7), calls=%async_computation | async-start | bytes 1048576 | tf_op jit(solution)/shard_map/all_to_all | solution.py:373
  18.8 0.0 copy-done.9
  18.8 0.0 copy-done
  18.8 0.0 copy-done.11
  18.8 0.0 copy-start.1
  18.8 1.1 copy-done.1
  19.9 0.0 copy-start.3
  19.9 1.6 %copy-done.3 = bf16[128,8192]{1,0:T(8,128)(2,1)S(1)} copy-done((bf16[128,8192]{1,0:T(8,128)(2,1)S(1)}, bf16[128,8192]{1,0:T(8,128)(2,1)}, u32[]{:S(2)}) %copy-start.3) | copy-done | bytes 2097176
  21.5 0.0 copy-start.10
  21.5 5.9 %own_part.1 = (bf16[8,1024,128]{2,1,0:T(8,128)(2,1)}, f32[8,8,1024]{2,1,0:T(8,128)S(1)}) custom-call(s32[16,64]{1,0:T(8,128)S(1)} %copy-done.11, bf16[128,128]{1,0:T(8,128)(2,1)S(1)} %copy-done.9, bf16[128,8192]{1,0:T(8,128)(2,1)S(1)} %copy-done.3, bf16[128,8192]{1,0:T(8,128)(2,1)S(1)} %copy-done, bf16[16,128,128]{2,1,0:T(8,128)(2,1)S(1)} %copy-done.1), custom_call_target="tpu_custom_call" | custom-call | flops 805306368 | bytes 7340032 | tf_op jit(solution)/shard_map/own_part/pallas_call | solution.py:331
  27.4 12.2 %all-to-all-done.source_ref = bf16[256,8,128]{2,1,0:T(8,128)(2,1)S(1)} async-done(((bf16[256,8,128]{2,1,0:T(8,128)(2,1)}), bf16[256,8,128]{2,1,0:T(8,128)(2,1)S(1)}, u32[]{:S(2)}, u32[]{:S(2)}) %all-to-all-start) | async-done | bytes 524320 | tf_op jit(solution)/shard_map/all_to_all | solution.py:373
  39.6 0.0 copy-start.4
  39.6 0.0 copy-done.10
  39.6 0.8 pick.1
  40.4 26.0 %all_to_all.20 = bf16[256,8,128]{2,1,0:T(8,128)(2,1)S(1)} all-to-all(bf16[256,8,128]{2,1,0:T(8,128)(2,1)S(1)} %pick.1), channel_id=1, replica_groups=mesh['sp'=16,'blk'=16] {'blk','sp'}, dimensions={0} | all-to-all | bytes 1048576 | tf_op jit(solution)/shard_map/all_to_all | solution.py:373
  66.4 0.0 copy-start.5
  66.4 0.0 copy-done.4
  66.4 0.0 copy-start.2
  66.4 4.2 %listed_part.1 = (bf16[16,128,128]{2,1,0:T(8,128)(2,1)S(1)}, f32[8,8,1024]{2,1,0:T(8,128)S(1)}) custom-call(s32[256]{0:T(256)S(1)} %bitcast.13, bf16[128,128]{1,0:T(8,128)(2,1)S(1)} %copy-done.9, bf16[8,1024,128]{2,1,0:T(8,128)(2,1)S(1)} %copy-done.4, bf16[128,8192]{1,0:T(8,128)(2,1)S(1)} %copy-done, bf16[16,128,128]{2,1,0:T(8,128)(2,1)S(1)} %bitcast.9, ...), custom_call_target="tpu_custom_call" | custom-call | flops 1073741824 | bytes 6291456 | tf_op jit(solution)/shard_map/listed_part/pallas_call | solution.py:344
  70.6 0.0 copy-done.5
  70.6 0.0 copy-start.8
  70.6 0.8 copy-done.8
  71.4 5.4 %all-to-all-start.2 = ((bf16[256,8,128]{2,1,0:T(8,128)(2,1)}), bf16[256,8,128]{2,1,0:T(8,128)(2,1)S(1)}, u32[]{:S(2)}, u32[]{:S(2)}) async-start(bf16[256,8,128]{2,1,0:T(8,128)(2,1)} %bitcast.11), calls=%async_computation.2 | async-start | bytes 1048576 | tf_op jit(solution)/shard_map/all_to_all | solution.py:373
  76.7 0.0 copy-done.2
  76.8 0.0 copy-start.6
  76.8 1.0 copy-done.6
  77.8 10.8 %rest_part.1 = (bf16[128,8192]{1,0:T(8,128)(2,1)}, bf16[128,8192]{1,0:T(8,128)(2,1)}, f32[16,128,128]{2,1,0:T(8,128)}) custom-call(s32[256]{0:T(256)S(1)} %bitcast.14, bf16[128,128]{1,0:T(8,128)(2,1)S(1)} %copy-done.9, bf16[8,1024,128]{2,1,0:T(8,128)(2,1)} %get-tuple-element.22.deq_ref, bf16[128,8192]{1,0:T(8,128)(2,1)S(1)} %copy-done, ...), custom_call_target="tpu_custom_call" | custom-call | flops 2684354560 | bytes 11534336 | tf_op jit(solution)/shard_map/rest_part/pallas_call | solution.py:359
  88.6 0.0 copy-start.7
  88.6 9.0 %all-to-all-done.2.part_ref = bf16[256,8,128]{2,1,0:T(8,128)(2,1)S(1)} async-done(((bf16[256,8,128]{2,1,0:T(8,128)(2,1)}), bf16[256,8,128]{2,1,0:T(8,128)(2,1)S(1)}, u32[]{:S(2)}, u32[]{:S(2)}) %all-to-all-start.2) | async-done | bytes 524320 | tf_op jit(solution)/shard_map/all_to_all | solution.py:373
  97.6 1.3 %accumulate.1 = bf16[256,8,128]{2,1,0:T(8,128)(2,1)S(1)} custom-call(s32[256]{0:T(256)S(1)} %bitcast.15, bf16[256,8,128]{2,1,0:T(8,128)(2,1)S(1)} %all-to-all-done.2.part_ref), custom_call_target="tpu_custom_call" | custom-call | tf_op jit(solution)/shard_map/accumulate/pallas_call | solution.py:278
  98.9 26.0 %all_to_all.21 = bf16[256,8,128]{2,1,0:T(8,128)(2,1)S(1)} all-to-all(bf16[256,8,128]{2,1,0:T(8,128)(2,1)S(1)} %accumulate.1), channel_id=1, replica_groups=mesh['sp'=16,'blk'=16] {'blk','sp'}, dimensions={0} | all-to-all | bytes 1048576 | tf_op jit(solution)/shard_map/all_to_all | solution.py:373
  124.9 0.0 copy-done.7
  124.9 0.8 finish.1
Async XLA Ops:
  0.6 18.1 %copy-start.9 = (bf16[128,128]{1,0:T(8,128)(2,1)S(1)}, bf16[128,128]{1,0:T(8,128)(2,1)}, u32[]{:S(2)}) copy-start(bf16[128,128]{1,0:T(8,128)(2,1)} %constant.2.clone.hadamard_ref) | copy-start | bytes 98308
  0.6 18.1 %copy-start = (bf16[128,8192]{1,0:T(8,128)(2,1)S(1)}, bf16[128,8192]{1,0:T(8,128)(2,1)}, u32[]{:S(2)}) copy-start(bf16[128,8192]{1,0:T(8,128)(2,1)} %grad_ref.5) | copy-start | bytes 6291460
  0.7 18.1 %copy-start.11 = (s32[16,64]{1,0:T(8,128)S(1)}, s32[16,64]{1,0:T(8,128)}, u32[]{:S(2)}) copy-start(s32[16,64]{1,0:T(8,128)} %exponent.1) | copy-start | bytes 12292
  3.1 36.5 %all-to-all-start = ((bf16[256,8,128]{2,1,0:T(8,128)(2,1)}), bf16[256,8,128]{2,1,0:T(8,128)(2,1)S(1)}, u32[]{:S(2)}, u32[]{:S(2)}) async-start(bf16[256,8,128]{2,1,0:T(8,128)(2,1)} %bitcast.7), calls=%async_computation | async-start | bytes 1048576 | tf_op jit(solution)/shard_map/all_to_all | solution.py:373
  18.8 1.1 copy-start.1
  19.9 1.6 %copy-start.3 = (bf16[128,8192]{1,0:T(8,128)(2,1)S(1)}, bf16[128,8192]{1,0:T(8,128)(2,1)}, u32[]{:S(2)}) copy-start(bf16[128,8192]{1,0:T(8,128)(2,1)} %query_ref.1) | copy-start | bytes 6291460
  21.5 18.1 %copy-start.10 = (s32[256,1]{0,1:T(1,128)S(1)}, s32[256,1]{0,1:T(1,128)}, u32[]{:S(2)}) copy-start(s32[256,1]{0,1:T(1,128)} %param.13) | copy-start | bytes 3076
  39.6 26.8 %copy-start.4 = (bf16[8,1024,128]{2,1,0:T(8,128)(2,1)S(1)}, bf16[8,1024,128]{2,1,0:T(8,128)(2,1)}, u32[]{:S(2)}) copy-start(bf16[8,1024,128]{2,1,0:T(8,128)(2,1)} %get-tuple-element.22.deq_ref) | copy-start | bytes 6291460
  66.4 4.2 %copy-start.5 = (bf16[256,8,128]{2,1,0:T(8,128)(2,1)}, bf16[256,8,128]{2,1,0:T(8,128)(2,1)S(1)}, u32[]{:S(2)}) copy-start(bf16[256,8,128]{2,1,0:T(8,128)(2,1)S(1)} %all_to_all.20) | copy-start | bytes 1572868
  66.4 10.4 %copy-start.2 = (bf16[16,128,128]{2,1,0:T(8,128)(2,1)S(1)}, bf16[16,128,128]{2,1,0:T(8,128)(2,1)}, u32[]{:S(2)}) copy-start(bf16[16,128,128]{2,1,0:T(8,128)(2,1)} %pack.1.pair_ref.own_ref) | copy-start | bytes 1572868
  70.6 0.8 copy-start.8
  71.4 26.2 %all-to-all-start.2 = ((bf16[256,8,128]{2,1,0:T(8,128)(2,1)}), bf16[256,8,128]{2,1,0:T(8,128)(2,1)S(1)}, u32[]{:S(2)}, u32[]{:S(2)}) async-start(bf16[256,8,128]{2,1,0:T(8,128)(2,1)} %bitcast.11), calls=%async_computation.2 | async-start | bytes 1048576 | tf_op jit(solution)/shard_map/all_to_all | solution.py:373
  76.8 1.0 copy-start.6
  88.6 36.3 %copy-start.7 = (f32[16,128,128]{2,1,0:T(8,128)S(1)}, f32[16,128,128]{2,1,0:T(8,128)}, u32[]{:S(2)}) copy-start(f32[16,128,128]{2,1,0:T(8,128)} %get-tuple-element.32.own_ref) | copy-start | bytes 3145732
